TPU v7x, 32 devices: a whole 2x2x4 slice. The times are simulated.
32 devices in a mesh: row: 4 (over z), col: 8 (over y, x, core).
Axes of the slice: x: 2, y: 2, z: 4, core: 2. Of those that a mesh axis runs over, the one named last changes fastest.
Arguments:
- covariance: float32 [16384, 16384], P('row', 'col'), may hold values from -6 to 6
- wind_direction: int32 [2, 16384], replicated, may hold values from 0 to 3
- wind_speed: int32 [2, 16384], replicated, may hold values from 0 to 7
- speed_table: float32 [2, 8], replicated, may hold values from 0.05 to 0.4
- diffusivity: float32 [128], replicated, may hold values from 0.005 to 0.05
Outputs:
- predicted_covariance: float32 [16384, 16384], P('row', 'col')
All inputs are finite; a program needn't handle non-finite values.
Results may differ from a plain program's by a relative error of at most 0.00002.
Values sent between devices are 32-bit elements; how exact they have to be, the bound alone decides.
No kernel may reach another device: no remote copies, remote signals or barrier semaphores. Data moves between devices by JAX's collectives and lax.ppermute only.
A program may use at most 448 MiB of HBM per device.

v0:
```python
import jax
import jax.numpy as jnp
from jax import lax
from jax.sharding import PartitionSpec as P

NLAT = 128
NLON = 128
SUBSTEPS = 2


def extended(array, sides, width):
    for axis, dim in sides:
        count, length = (lax.axis_size(axis), array.shape[dim])
        up = [(i, (i + 1) % count) for i in range(count - 1)]
        down = [(j, i) for i, j in up]
        last = lax.slice_in_dim(array, length - width, length, axis=dim)
        first = lax.slice_in_dim(array, 0, width, axis=dim)
        before = lax.ppermute(last, axis, up)
        after = lax.ppermute(first, axis, down)
        array = jnp.concatenate([before, array, after], axis=dim)
    return array


def build_coefficients(wind_direction, wind_speed, speed_table, diffusivity, nlat, nlon):
    substeps = wind_direction.shape[0]
    category_list = speed_table.shape[1]
    onehot = (wind_speed[:, :, None] == jnp.arange(category_list, dtype=jnp.int32)).astype(
        speed_table.dtype
    )
    lon_courant = jnp.sum(onehot * speed_table[0], axis=2).reshape(substeps, nlat, nlon)
    lat_courant = jnp.sum(onehot * speed_table[1], axis=2).reshape(substeps, nlat, nlon)
    eastward = (wind_direction % 2 == 0).astype(speed_table.dtype).reshape(substeps, nlat, nlon)
    northward = (wind_direction // 2 == 0).astype(speed_table.dtype).reshape(substeps, nlat, nlon)
    diffusion = diffusivity[None, :, None]
    center = 1.0 - lon_courant - lat_courant - 4.0 * diffusion
    western = lon_courant * eastward + diffusion
    eastern = lon_courant * (1.0 - eastward) + diffusion
    southern = lat_courant * northward + diffusion
    northern = lat_courant * (1.0 - northward) + diffusion
    return jnp.stack([center, western, eastern, southern, northern], axis=1)


def substep(tracer, weights):
    span_length = tracer.shape[0]
    middle = tracer[1 : span_length - 1]
    southern = tracer[0 : span_length - 2]
    northern = tracer[2:span_length]
    return (
        weights[0] * middle
        + weights[1] * jnp.roll(middle, 1, axis=1)
        + weights[2] * jnp.roll(middle, -1, axis=1)
        + weights[3] * southern
        + weights[4] * northern
    )


def advance_rows(padded, table_padded, lat_start, lat_count):
    substeps = table_padded.shape[0]
    tracer = padded
    for section_idx in range(substeps):
        span_length = lat_count + 2 * (substeps - 1 - section_idx)
        weights = lax.dynamic_slice_in_dim(
            table_padded[section_idx], lat_start + section_idx + 1, span_length, 1
        )
        tracer = substep(tracer, weights[..., None])
    return tracer


def advance_flat(padded, table_padded, lat_start, lat_count, nlon):
    substeps = table_padded.shape[0]
    tracer = padded
    for section_idx in range(substeps):
        span_length = lat_count + 2 * (substeps - 1 - section_idx)
        weights = lax.dynamic_slice_in_dim(
            table_padded[section_idx], lat_start + section_idx + 1, span_length, 1
        )
        weights = weights.reshape(weights.shape[0], 1, span_length * nlon)
        total = tracer.shape[1]
        middle = tracer[:, nlon : total - nlon]
        southern = tracer[:, 0 : total - 2 * nlon]
        northern = tracer[:, 2 * nlon : total]
        longitude = (jnp.arange(span_length * nlon, dtype=jnp.int32) % nlon)[None, :]
        western = jnp.where(
            longitude == 0, jnp.roll(middle, 1 - nlon, axis=1), jnp.roll(middle, 1, axis=1)
        )
        eastern = jnp.where(
            longitude == nlon - 1, jnp.roll(middle, nlon - 1, axis=1), jnp.roll(middle, -1, axis=1)
        )
        tracer = (
            weights[0] * middle
            + weights[1] * western
            + weights[2] * eastern
            + weights[3] * southern
            + weights[4] * northern
        )
    return tracer


def local(covariance, wind_direction, wind_speed, speed_table, diffusivity):
    weight_table = build_coefficients(
        wind_direction, wind_speed, speed_table, diffusivity, NLAT, NLON
    )
    table_padded = jnp.pad(weight_table, ((0, 0), (0, 0), (SUBSTEPS, SUBSTEPS), (0, 0)))
    rows_tile, cols_tile = covariance.shape
    lat_rows = rows_tile // NLON
    lat_start = lax.axis_index("row") * lat_rows
    tracer = covariance.reshape(lat_rows, NLON, cols_tile)
    padded = extended(tracer, (("row", 0),), SUBSTEPS)
    advected = advance_rows(padded, table_padded, lat_start, lat_rows).reshape(rows_tile, cols_tile)
    latitude_columns = cols_tile // NLON
    column_offset = lax.axis_index("col") * latitude_columns
    column_padded = extended(advected, (("col", 1),), SUBSTEPS * NLON)
    predicted_covariance = advance_flat(
        column_padded, table_padded, column_offset, latitude_columns, NLON
    )
    return predicted_covariance


def solution(mesh):
    return jax.shard_map(
        local,
        mesh=mesh,
        in_specs=(P("row", "col"), P(), P(), P(), P()),
        out_specs=P("row", "col"),
        check_vma=False,
    )
```

profile of v0, /device:TPU:25, one launch (start us, length us, event | category | flops | bytes accessed | tf_op | source)
XLA Modules:
  0.0 843.2 jit_solution(349393629501530375)
XLA Ops:
  0.0 4.8 fusion.54
  4.8 2.2 collective-permute-start.1
  7.0 1.3 collective-permute-start
  9.0 1.7 select_reduce_fusion.1
  11.5 1.5 compare_bitcast_fusion
  16.1 35.3 %collective-permute-done.1 = f32[2,128,2048]{2,1,0:T(8,128)S(1)} collective-permute-done((f32[2,128,2048]{2,1,0:T(8,128)}, f32[2,128,2048]{2,1,0:T(8,128)S(1)}, u32[]{:S(2)}, u32[]{:S(2)}) %collective-permute-start.1) | collective-permute-done | bytes 2097184 | tf_op jit(solution)/shard_map/ppermute | solution.py:19
  51.4 3.9 collective-permute-done
  55.4 24.7 %pad_maximum_fusion.1 = f32[36,128,2048]{2,1,0:T(8,128)} fusion(f32[2,128,2048]{2,1,0:T(8,128)S(1)} %collective-permute-done.1, f32[32,128,2048]{2,1,0:T(8,128)} %bitcast.101, f32[2,128,2048]{2,1,0:T(8,128)} %collective-permute-done), kind=kLoop, calls=%fused_computation.6 | loop fusion | flops 18874368 | bytes 75497472 | tf_op jit(solution)/shard_map/concatenate | solution.py:20
  80.1 46.1 %fusion.50 = (f32[34,127,2048]{2,1,0:T(8,128)}, f32[34,127,2048]{2,1,0:T(8,128)}) fusion(f32[36,128,2048]{2,1,0:T(8,128)} %pad_maximum_fusion.1), kind=kLoop, calls=%fused_computation.121 | loop fusion | bytes 141492224 | tf_op jit(solution)/shard_map/jit(_roll_static)/slice | solution.py:51
  126.2 70.2 %fusion.10 = f32[34,128,2048]{2,1,0:T(8,128)} fusion(f32[2,128,2048]{2,1,0:T(8,128)S(1)} %collective-permute-done.1, f32[32,128,2048]{2,1,0:T(8,128)} %bitcast.102, f32[2,128,2048]{2,1,0:T(8,128)} %collective-permute-done, f32[36,128,2048]{2,1,0:T(8,128)} %pad_maximum_fusion.1, f32[34,127,2048]{2,1,0:T(8,128)} %get-tuple-element.20, ...), kind=kLoop, calls=%fused_computation.18 | loop fusion | flops 151519232 | bytes 179885056 | tf_op jit(solution)/shard_map/add | solution.py:49
  196.4 2.7 fusion.52
  199.0 46.2 %fusion.51 = (f32[32,127,2048]{2,1,0:T(8,128)}, f32[32,127,2048]{2,1,0:T(8,128)}) fusion(f32[34,128,2048]{2,1,0:T(8,128)} %fusion.10), kind=kLoop, calls=%fused_computation.122 | loop fusion | bytes 133169152 | tf_op jit(solution)/shard_map/jit(_roll_static)/slice | solution.py:51
  245.2 63.3 %fusion.18 = f32[32,128,2048]{2,1,0:T(8,128)} fusion(f32[34,128,2048]{2,1,0:T(8,128)} %fusion.10, f32[32,127,2048]{2,1,0:T(8,128)} %get-tuple-element.22, f32[32,1,2048]{2,1,0:T(1,128)S(1)} %get-tuple-element.24, f32[32,1,2048]{2,1,0:T(1,128)S(1)} %get-tuple-element.23, f32[32,127,2048]{2,1,0:T(8,128)} %get-tuple-element.21, ...), kind=kLoop, calls=%fused_computation.36 | loop fusion | flops 92274688 | bytes 201408512 | tf_op jit(solution)/shard_map/add | solution.py:49
  308.5 7.3 fusion.53
  315.8 4.9 collective-permute-start.2
  320.7 2.3 collective-permute-start.3
  323.6 1.4 dynamic-slice_bitcast_fusion.19
  325.9 40.6 %collective-permute-done.2 = f32[4096,256]{1,0:T(8,128)} collective-permute-done((f32[4096,256]{1,0:T(8,128)}, f32[4096,256]{1,0:T(8,128)}, u32[]{:S(2)}, u32[]{:S(2)}) %collective-permute-start.2) | collective-permute-done | bytes 4194336 | tf_op jit(solution)/shard_map/ppermute | solution.py:18
  366.5 46.6 %collective-permute-done.3 = f32[4096,256]{1,0:T(8,128)} collective-permute-done((f32[4096,256]{1,0:T(8,128)}, f32[4096,256]{1,0:T(8,128)}, u32[]{:S(2)}, u32[]{:S(2)}) %collective-permute-start.3) | collective-permute-done | bytes 4194336 | tf_op jit(solution)/shard_map/ppermute | solution.py:19
  413.1 27.9 %pad_maximum_fusion = f32[4096,2560]{1,0:T(8,128)} fusion(f32[4096,256]{1,0:T(8,128)} %collective-permute-done.3, f32[4096,2048]{1,0:T(8,128)} %bitcast.99, f32[4096,256]{1,0:T(8,128)} %collective-permute-done.2), kind=kLoop, calls=%fused_computation | loop fusion | flops 20971520 | bytes 83886080 | tf_op jit(solution)/shard_map/concatenate | solution.py:20
  440.9 51.3 %fusion.44 = (f32[4096,2303]{1,0:T(8,128)}, f32[4096,2303]{1,0:T(8,128)}) fusion(f32[4096,2560]{1,0:T(8,128)} %pad_maximum_fusion), kind=kLoop, calls=%fused_computation.115 | loop fusion | bytes 150929408 | tf_op jit(solution)/shard_map/jit(_roll_static)/slice | solution.py:87
  492.2 51.2 %fusion.45 = (f32[4096,2177]{1,0:T(8,128)}, f32[4096,2177]{1,0:T(8,128)}) fusion(f32[4096,2560]{1,0:T(8,128)} %pad_maximum_fusion), kind=kLoop, calls=%fused_computation.116 | loop fusion | bytes 142671872 | tf_op jit(solution)/shard_map/jit(_roll_static)/slice | solution.py:87
  543.4 1.7 slice.350
  545.1 3.0 slice.344
  548.2 3.6 slice.347
  551.8 3.5 slice.345
  555.3 104.2 %fusion.3 = f32[4096,2304]{1,0:T(8,128)} fusion(f32[4096,2560]{1,0:T(8,128)} %pad_maximum_fusion, f32[4096,127]{1,0:T(8,128)} %slice.344, f32[4096,2177]{1,0:T(8,128)} %get-tuple-element.10, f32[4096,2303]{1,0:T(8,128)} %get-tuple-element.8, f32[4096,1]{1,0:T(8,128)} %slice.345, f32[4096,2177]{1,0:T(8,128)} %get-tuple-element.9, f32[4096,127]{1,0:T(8,128)} %slice.347, ...), kind=kLoop, calls=%fused_computation.5 | loop fusion | flops 160432128 | bytes 268486144 | tf_op jit(solution)/shard_map/add | solution.py:90
  659.5 4.2 fusion.47
  663.7 4.9 fusion.48
  668.6 44.4 %fusion.46 = (f32[4096,2047]{1,0:T(8,128)}, f32[4096,2047]{1,0:T(8,128)}) fusion(f32[4096,2304]{1,0:T(8,128)} %fusion.3), kind=kLoop, calls=%fused_computation.117 | loop fusion | bytes 134152192 | tf_op jit(solution)/shard_map/jit(_roll_static)/slice | solution.py:87
  713.0 44.4 %fusion.49 = (f32[4096,1921]{1,0:T(8,128)}, f32[4096,1921]{1,0:T(8,128)}) fusion(f32[4096,2304]{1,0:T(8,128)} %fusion.3), kind=kLoop, calls=%fused_computation.120 | loop fusion | bytes 125894656 | tf_op jit(solution)/shard_map/jit(_roll_static)/slice | solution.py:87
  757.4 85.8 %fusion.14 = f32[4096,2048]{1,0:T(8,128)} fusion(f32[4096,2304]{1,0:T(8,128)} %fusion.3, f32[4096,127]{1,0:T(8,128)} %get-tuple-element.16, f32[4096,1921]{1,0:T(8,128)} %get-tuple-element.18, f32[4096,2047]{1,0:T(8,128)} %get-tuple-element.12, f32[4096,1]{1,0:T(8,128)} %get-tuple-element.14, f32[4096,1921]{1,0:T(8,128)} %get-tuple-element.17, ...), kind=kLoop, calls=%fused_computation.29 | loop fusion | flops 125829120 | bytes 268480512 | tf_op jit(solution)/shard_map/add | solution.py:90
  (31 shorter events, 6.0 us)
Async XLA Ops:
  4.8 46.7 %collective-permute-start.1 = (f32[2,128,2048]{2,1,0:T(8,128)}, f32[2,128,2048]{2,1,0:T(8,128)S(1)}, u32[]{:S(2)}, u32[]{:S(2)}) collective-permute-start(f32[2,128,2048]{2,1,0:T(8,128)} %bitcast.8), channel_id=1, source_target_pairs={{8,0},{16,8},{24,16},{9,1},{17,9},{25,17},{10,2},{18,10},{26,18},{... | collective-permute-start | bytes 6291464 | tf_op jit(solution)/shard_map/ppermute | solution.py:19
  7.0 48.4 %collective-permute-start = (f32[2,128,2048]{2,1,0:T(8,128)}, f32[2,128,2048]{2,1,0:T(8,128)}, u32[]{:S(2)}, u32[]{:S(2)}) collective-permute-start(f32[2,128,2048]{2,1,0:T(8,128)} %bitcast.6), channel_id=1, source_target_pairs={{0,8},{8,16},{16,24},{1,9},{9,17},{17,25},{2,10},{10,18},{18,26},{... | collective-permute-start | bytes 6291464 | tf_op jit(solution)/shard_map/ppermute | solution.py:18
  16.1 35.4 %copy-start = (f32[1,5,132,128]{3,2,0,1:T(8,128)}, f32[1,5,132,128]{3,2,0,1:T(8,128)S(1)}, u32[]{:S(2)}) copy-start(f32[1,5,132,128]{3,2,0,1:T(8,128)S(1)} %get-tuple-element.30) | copy-start | bytes 1013764
  16.1 39.3 %copy-start.1 = (f32[1,5,132,128]{3,2,0,1:T(8,128)}, f32[1,5,132,128]{3,2,0,1:T(8,128)S(1)}, u32[]{:S(2)}) copy-start(f32[1,5,132,128]{3,2,0,1:T(8,128)S(1)} %get-tuple-element.29) | copy-start | bytes 1013764
  315.8 50.6 %collective-permute-start.2 = (f32[4096,256]{1,0:T(8,128)}, f32[4096,256]{1,0:T(8,128)}, u32[]{:S(2)}, u32[]{:S(2)}) collective-permute-start(f32[4096,256]{1,0:T(8,128)} %get-tuple-element.25), channel_id=1, source_target_pairs={{0,1},{1,2},{2,3},{3,4},{4,5},{5,6},{6,7},{8,9},{9,10},{10,11},{11... | collective-permute-start | bytes 12582920 | tf_op jit(solution)/shard_map/ppermute | solution.py:18
  320.7 92.3 %collective-permute-start.3 = (f32[4096,256]{1,0:T(8,128)}, f32[4096,256]{1,0:T(8,128)}, u32[]{:S(2)}, u32[]{:S(2)}) collective-permute-start(f32[4096,256]{1,0:T(8,128)} %get-tuple-element.26), channel_id=1, source_target_pairs={{1,0},{2,1},{3,2},{4,3},{5,4},{6,5},{7,6},{9,8},{10,9},{11,10},{12... | collective-permute-start | bytes 12582920 | tf_op jit(solution)/shard_map/ppermute | solution.py:19
  713.0 44.4 %copy-start.2 = (f32[2048]{0:T(1024)S(1)}, f32[2048]{0:T(1024)}, u32[]{:S(2)}) copy-start(f32[2048]{0:T(1024)} %get-tuple-element.31) | copy-start | bytes 24580
  713.0 44.4 %copy-start.3 = (f32[2048]{0:T(1024)S(1)}, f32[2048]{0:T(1024)}, u32[]{:S(2)}) copy-start(f32[2048]{0:T(1024)} %get-tuple-element.32) | copy-start | bytes 24580
  713.0 44.4 %copy-start.4 = (f32[2048]{0:T(1024)S(1)}, f32[2048]{0:T(1024)}, u32[]{:S(2)}) copy-start(f32[2048]{0:T(1024)} %get-tuple-element.33) | copy-start | bytes 24580
  713.0 44.4 %copy-start.5 = (f32[2048]{0:T(1024)S(1)}, f32[2048]{0:T(1024)}, u32[]{:S(2)}) copy-start(f32[2048]{0:T(1024)} %get-tuple-element.34) | copy-start | bytes 24580
  713.0 44.4 %copy-start.6 = (f32[2048]{0:T(1024)S(1)}, f32[2048]{0:T(1024)}, u32[]{:S(2)}) copy-start(f32[2048]{0:T(1024)} %get-tuple-element.35) | copy-start | bytes 24580
  713.0 44.4 %copy-start.7 = (pred[2048]{0:T(1024)(128)(4,1)S(1)}, pred[2048]{0:T(1024)(128)(4,1)}, u32[]{:S(2)}) copy-start(pred[2048]{0:T(1024)(128)(4,1)} %get-tuple-element.55) | copy-start | bytes 6148
  713.0 44.4 %copy-start.8 = (pred[2048]{0:T(1024)(128)(4,1)S(1)}, pred[2048]{0:T(1024)(128)(4,1)}, u32[]{:S(2)}) copy-start(pred[2048]{0:T(1024)(128)(4,1)} %get-tuple-element.56) | copy-start | bytes 6148
where the time goes:
time: 844 us; the launch traced here: 843 us
  other arithmetic  384 us (45%)
  local copies, waits for them, and re-layouts  322 us (38%)
  waiting for transfers between devices  126 us (15%)
  starting transfers between devices  10.7 us (1%)
    add x2, other arithmetic, advance_flat(): weights[0] * middle + weights[1] * western + weights[2] * eastern  190 us
    add x2, other arithmetic, substep(): weights[0] * middle + weights[1] * jnp.roll(middle, 1, axis=1)  134 us
    slice x4, local copies, waits for them, and re-layouts, advance_flat(): jnp.roll(middle, nlon - 1, axis=1)  104 us
    slice x4, local copies, waits for them, and re-layouts, advance_flat(): jnp.roll(middle, -1, axis=1)  102 us
    slice x3, local copies, waits for them, and re-layouts, substep(): jnp.roll(middle, -1, axis=1)  94.9 us
    ppermute x2, waiting for transfers between devices, extended(): after = lax.ppermute(first, axis, down)  81.9 us
    concatenate x2, other arithmetic, extended(): array = jnp.concatenate([before, array, after], axis=dim)  52.6 us
    ppermute x2, waiting for transfers between devices, extended(): before = lax.ppermute(last, axis, up)  44.5 us
  transfers between devices with their start and end apart: 4, of which 4 were waited for; matrix products, arithmetic and copies ran while one was open for 1% of the time, Pallas kernels for 0%

commit v1 on v0

v1 whole, which is shorter than its diff:
```python
import functools

import jax
import jax.numpy as jnp
from jax import lax
from jax.experimental import pallas as pl
from jax.experimental.pallas import tpu as pltpu
from jax.sharding import PartitionSpec as P

NLAT = 128
NLON = 128
LANES = 128
PAD = 8
GROUPS = 2
F32 = jnp.float32
ANY = pl.BlockSpec(memory_space=pl.ANY)


def params(mib=56):
    return pltpu.CompilerParams(vmem_limit_bytes=mib << 20)


def cost(flops, size):
    return pl.CostEstimate(flops=flops, bytes_accessed=size, transcendentals=0)


def weights_kernel(rows, cols, wd, ws, table, diff, wr, wc, s_wd, s_ws, s_k, tile):
    def five(first, count, sub):
        for i in range(count):
            lat = jnp.clip(first + i, 0, NLAT - 1)
            at = pl.ds(pl.multiple_of(lat * NLON, NLON), NLON)
            s_wd[i : i + 1, :] = wd[sub : sub + 1, at]
            s_ws[i : i + 1, :] = ws[sub : sub + 1, at]
            s_k[i : i + 1, :] = jnp.full((1, LANES), diff[lat], F32)
        size = -(-count // 8) * 8
        speed, way, k = s_ws[:size, :], s_wd[:size, :], s_k[:size, :]
        u = v = jnp.zeros((size, LANES), F32)
        for c in range(table.shape[1]):
            u = jnp.where(speed == c, table[0, c], u)
            v = jnp.where(speed == c, table[1, c], v)
        lat = first + lax.broadcasted_iota(jnp.int32, (size, LANES), 0)
        keep = jnp.logical_and(lat >= 0, lat < NLAT)
        east = (way & 1) == 0
        north = way < 2
        out = [
            1.0 - u - v - 4.0 * k,
            jnp.where(east, u, 0.0) + k,
            jnp.where(east, 0.0, u) + k,
            jnp.where(north, v, 0.0) + k,
            jnp.where(north, 0.0, v) + k,
        ]
        return [jnp.where(keep, o, 0.0) for o in out]

    lat_row = lax.axis_index("row") * rows
    lat_col = lax.axis_index("col") * cols
    count = rows + 4
    w = five(lat_row - 3, count, 0) + five(lat_row - 4, count, 1)
    tile[...] = jnp.zeros_like(tile)
    for g in range(wr.shape[0]):
        for k in range(10):
            tile[8 * k : 8 * k + 8, :] = w[k][8 * g : 8 * g + 8, :]
        wr[g] = tile[...].T
    for sub in range(2):
        for k, o in enumerate(five(lat_col - 1, cols + 2, sub)):
            wc[5 * sub + k, : o.shape[0], :] = o


def weights_call(rows, cols, wd, ws, table, diff):
    most = -(-(max(rows, cols) + 4) // 8) * 8
    groups = -(-(rows + 4) // 8)
    smem = pl.BlockSpec(memory_space=pltpu.SMEM)
    vmem = pl.BlockSpec(memory_space=pltpu.VMEM)
    return pl.pallas_call(
        functools.partial(weights_kernel, rows, cols),
        in_specs=[vmem, vmem, smem, smem],
        out_specs=[vmem, vmem],
        out_shape=[
            jax.ShapeDtypeStruct((groups, NLON, LANES), F32),
            jax.ShapeDtypeStruct((10, -(-(cols + 2) // 8) * 8, LANES), F32),
        ],
        scratch_shapes=[
            pltpu.VMEM((most, LANES), jnp.int32),
            pltpu.VMEM((most, LANES), jnp.int32),
            pltpu.VMEM((most, LANES), F32),
            pltpu.VMEM((LANES, LANES), F32),
        ],
        compiler_params=params(),
        cost_estimate=cost(100000, 1 << 20),
    )(wd, ws, table, diff)


def lane_weights(wr, index, row, sub):
    w = wr[index // 8, pl.ds(row, 8), :]
    if isinstance(index, int):
        lane = [8 * (5 * sub + k) + index % 8 for k in range(5)]
    else:
        w = pltpu.roll(w, LANES - lax.rem(index, 8), 1)
        lane = [8 * (5 * sub + k) for k in range(5)]
    return [jnp.broadcast_to(w[:, a : a + 1], (8, LANES)) for a in lane]


def edge_kernel(count, first, wr, a, b, left, right, ga, gb):
    side = pl.program_id(0)
    sub_row = lax.broadcasted_iota(jnp.int32, (8, LANES), 0)

    def around(load, j):
        mid = load(8 * j)
        if j == 0:
            west = jnp.where(sub_row == 0, pltpu.roll(load(120), 1, 0), pltpu.roll(mid, 1, 0))
        else:
            west = load(8 * j - 1)
        if j == 15:
            east = jnp.where(sub_row == 7, pltpu.roll(load(0), 7, 0), pltpu.roll(mid, 7, 0))
        else:
            east = load(8 * j + 1)
        return mid, west, east

    @pl.loop(0, count + 2)
    def _(i):
        base = pl.multiple_of(i * 128, 128)
        for j in range(16):
            w = lane_weights(wr, first + i + 2, 8 * j, 0)
            for f, g in ((a, ga), (b, gb)):
                mid, west, east = around(lambda r: f[pl.ds(base + 128 + r, 8), :], j)
                so, no = f[pl.ds(base + 8 * j, 8), :], f[pl.ds(base + 256 + 8 * j, 8), :]
                g[pl.ds(base + 8 * j, 8), :] = w[0] * mid + w[1] * west + w[2] * east + w[3] * so + w[4] * no

    def second(out):
        @pl.loop(0, count)
        def _(i):
            base = pl.multiple_of(i * 128, 128)
            for j in range(16):
                w = lane_weights(wr, first + i + 4, 8 * j, 1)
                for c, g in enumerate((ga, gb)):
                    mid, west, east = around(lambda r: g[pl.ds(base + 128 + r, 8), :], j)
                    so, no = g[pl.ds(base + 8 * j, 8), :], g[pl.ds(base + 256 + 8 * j, 8), :]
                    out[pl.ds(base + 8 * j, 8), c * LANES : (c + 1) * LANES] = (
                        w[0] * mid + w[1] * west + w[2] * east + w[3] * so + w[4] * no
                    )

    pl.when(side == 0)(lambda: second(left))
    pl.when(side == 1)(lambda: second(right))


def edge_call(cov, wr, first, count, inside=0):
    size, wide = (count + 4) * 128, cov.shape[1]
    start = (first - 2 - inside) * 128
    spec = lambda at: pl.BlockSpec(
        (pl.Element(size), pl.Element(LANES)), lambda side: (start, LANES * (at + side * (wide // LANES - 2)))
    )
    out = jax.ShapeDtypeStruct((count * 128, 2 * LANES), F32)
    return pl.pallas_call(
        functools.partial(edge_kernel, count, first),
        grid=(2,),
        in_specs=[pl.BlockSpec(wr.shape, lambda s: (0, 0, 0)), spec(0), spec(1)],
        out_specs=[pl.BlockSpec(out.shape, lambda s: (0, 0))] * 2,
        out_shape=[out, out],
        scratch_shapes=[pltpu.VMEM(((count + 2) * 128, LANES), F32)] * 2,
        compiler_params=params(),
        cost_estimate=cost(count * 128 * 512 * 18, count * 128 * 512 * 8),
    )(wr, cov, cov)


def roll(x, k):
    return pltpu.roll(x, k, 1)


def one_lat(tiles, slot, mode, index, f_ref, f_base, o_ref, o_base, wr, wc, F, G):
    Fs, F1, F2 = F[slot], F[(slot - 1) % 4], F[(slot - 2) % 4]
    G1, G2, G3 = G[(slot - 1) % 4], G[(slot - 2) % 4], G[(slot - 3) % 4]

    @pl.loop(0, 16 // GROUPS)
    def _(j):
        rs = [pl.multiple_of(j * 8 * GROUPS + 8 * i, 8) for i in range(GROUPS)]
        w0 = [lane_weights(wr, index, r, 0) for r in rs] if mode >= 1 else None
        w1 = [lane_weights(wr, index, r, 1) for r in rs] if mode >= 2 else None

        def first(c):
            out = []
            for i, r in enumerate(rs):
                x = f_ref[pl.ds(f_base + r, 8), c * LANES : (c + 1) * LANES]
                Fs[c, pl.ds(PAD + r, 8), :] = x
                if mode >= 1:
                    w = w0[i]
                    g = (
                        w[0] * F1[c, pl.ds(PAD + r, 8), :]
                        + w[1] * F1[c, pl.ds(PAD - 1 + r, 8), :]
                        + w[2] * F1[c, pl.ds(PAD + 1 + r, 8), :]
                        + w[3] * F2[c, pl.ds(PAD + r, 8), :]
                        + w[4] * x
                    )
                    G1[c, pl.ds(PAD + r, 8), :] = g
                    out.append(g)
            return out

        def second(c):
            g = first(c)
            return [
                w[0] * G2[c, pl.ds(PAD + r, 8), :]
                + w[1] * G2[c, pl.ds(PAD - 1 + r, 8), :]
                + w[2] * G2[c, pl.ds(PAD + 1 + r, 8), :]
                + w[3] * G3[c, pl.ds(PAD + r, 8), :]
                + w[4] * g[i]
                for i, (r, w) in enumerate(zip(rs, w1))
            ]

        def across(sub, c, mid, so, no):
            W = [jnp.broadcast_to(wc[5 * sub + k, c + 1 : c + 2, :], (8, LANES)) for k in range(5)]
            out = []
            for i in range(GROUPS):
                t = None
                if mid is not None:
                    t = W[0] * mid[i] + W[1] * roll(mid[i], 1) + W[2] * roll(mid[i], LANES - 1)
                if so is not None:
                    t = W[3] * so[i] if t is None else t + W[3] * so[i]
                if no is not None:
                    t = W[4] * no[i] if t is None else t + W[4] * no[i]
                out.append(t)
            return out

        if mode < 2:
            for c in range(tiles):
                first(c)
            return
        h, u = {-2: None, -1: None}, {-2: None}
        for c in range(tiles + 2):
            h[c] = second(c) if c < tiles else None
            u[c - 1] = across(0, c - 1, h[c - 1], h[c - 2], h[c])
            if c >= 2:
                o = across(1, c - 2, u[c - 2], u[c - 3], u[c - 1])
                for i, r in enumerate(rs):
                    o_ref[pl.ds(o_base + r, 8), (c - 2) * LANES : (c - 1) * LANES] = o[i]

    for ring in (Fs, G1) if mode >= 1 else (Fs,):
        ring[:, PAD - 1 : PAD, :] = ring[:, PAD + 127 : PAD + 128, :]
        ring[:, PAD + 128 : PAD + 129, :] = ring[:, PAD : PAD + 1, :]


def main_kernel(tiles, wr, wc, f_ref, o_ref, *ring):
    F, G = ring[:4], ring[4:8]
    t = pl.program_id(0)

    def four(modes):
        for q in range(4):
            one_lat(tiles, q, modes[q], 4 * t + q + 2, f_ref, 128 * q, o_ref, 128 * q, wr, wc, F, G)

    pl.when(t == 0)(lambda: four((0, 0, 1, 1)))
    pl.when(t > 0)(lambda: four((2, 2, 2, 2)))


def rings(tiles):
    return [pltpu.VMEM((tiles, 128 + 2 * PAD, LANES), F32)] * 8


def main_call(cov, wr, wc):
    rows, wide = cov.shape[0] // 128, cov.shape[1]
    return pl.pallas_call(
        functools.partial(main_kernel, wide // LANES),
        grid=(rows // 4,),
        in_specs=[
            pl.BlockSpec(wr.shape, lambda s: (0, 0, 0)),
            pl.BlockSpec(wc.shape, lambda s: (0, 0, 0)),
            pl.BlockSpec((512, wide), lambda s: (s, 0)),
        ],
        out_specs=pl.BlockSpec(
            (pl.Element(512), pl.Element(wide)), lambda s: (128 * jnp.maximum(4 * s - 2, 2), 0)
        ),
        out_shape=jax.ShapeDtypeStruct(cov.shape, F32),
        scratch_shapes=rings(wide // LANES),
        compiler_params=params(),
        cost_estimate=cost(cov.size * 36, cov.size * 8),
    )(wr, wc, cov)


def rim_kernel(tiles, rows, wr, wc, before, after, c_ref, _, o_ref, *ring):
    F, G = ring[:4], ring[4:8]
    side = pl.program_id(0)

    def six(refs, index):
        for q, (mode, (ref, base)) in enumerate(zip((0, 0, 1, 1, 2, 2), refs)):
            one_lat(tiles, q % 4, mode, index + q, ref, base, o_ref, 128 * (q - 4), wr, wc, F, G)

    own = [(c_ref, 128 * q) for q in range(4)]
    pl.when(side == 0)(lambda: six([(before, 0), (before, 128)] + own, 0))
    pl.when(side == 1)(lambda: six(own + [(after, 0), (after, 128)], rows - 2))


def rim_call(cov, wr, wc, before, after, out):
    rows, wide = cov.shape[0] // 128, cov.shape[1]
    halo = pl.BlockSpec((256, wide), lambda s: (0, 0))
    return pl.pallas_call(
        functools.partial(rim_kernel, wide // LANES, rows),
        grid=(2,),
        in_specs=[
            pl.BlockSpec(wr.shape, lambda s: (0, 0, 0)),
            pl.BlockSpec(wc.shape, lambda s: (0, 0, 0)),
            halo,
            halo,
            pl.BlockSpec((512, wide), lambda s: (s * (rows // 4 - 1), 0)),
            ANY,
        ],
        out_specs=pl.BlockSpec((256, wide), lambda s: (s * (rows // 2 - 1), 0)),
        out_shape=jax.ShapeDtypeStruct(cov.shape, F32),
        scratch_shapes=rings(wide // LANES),
        input_output_aliases={5: 0},
        compiler_params=params(),
        cost_estimate=cost(cov.size * 4, cov.size),
    )(wr, wc, before, after, cov, out)


def halo_kernel(tiles, wc, low, high, o_in, o_ref):
    side = pl.program_id(0)
    height = o_ref.shape[0]

    def weight(sub, k, lat):
        return jnp.broadcast_to(wc[5 * sub + k, lat + 1 : lat + 2, :], (8, LANES))

    def add(ref, near, far, outer, edge, inner, way, at_edge, at_inner):
        a = [weight(0, k, outer) for k in (0, 1, 2, way)]
        b = weight(0, way, edge)
        d = [weight(1, k, edge) for k in (0, 1, 2, way)]
        e = weight(1, way, inner)

        @pl.loop(0, height // 32)
        def _(i):
            for j in range(4):
                at = pl.ds(pl.multiple_of(i * 32 + 8 * j, 8), 8)
                f1, f2 = ref[at, near : near + LANES], ref[at, far : far + LANES]
                u1 = a[0] * f1 + a[1] * roll(f1, 1) + a[2] * roll(f1, LANES - 1) + a[3] * f2
                u0 = b * f1
                o_ref[at, at_edge : at_edge + LANES] = o_in[at, at_edge : at_edge + LANES] + (
                    d[0] * u0 + d[1] * roll(u0, 1) + d[2] * roll(u0, LANES - 1) + d[3] * u1
                )
                o_ref[at, at_inner : at_inner + LANES] = o_in[at, at_inner : at_inner + LANES] + e * u0

    pl.when(side == 0)(lambda: add(low, LANES, 0, -1, 0, 1, 3, 0, LANES))
    pl.when(side == 1)(lambda: add(high, 0, LANES, tiles, tiles - 1, tiles - 2, 4, LANES, 0))


def halo_call(out, wc, low, high, blocks, height):
    wide = out.shape[1]
    first, step, count = blocks
    last = wide // 256 - 1
    at = pl.BlockSpec((height, 256), lambda s, i: (first + step * i, s * last))
    return pl.pallas_call(
        functools.partial(halo_kernel, wide // LANES),
        grid=(2, count),
        in_specs=[
            pl.BlockSpec(wc.shape, lambda s, i: (0, 0, 0)),
            pl.BlockSpec((height, 256), lambda s, i: (jnp.where(s == 0, i, count - 1), 0)),
            pl.BlockSpec((height, 256), lambda s, i: (jnp.where(s == 1, i, 0), 0)),
            at,
        ],
        out_specs=at,
        out_shape=jax.ShapeDtypeStruct(out.shape, F32),
        input_output_aliases={3: 0},
        compiler_params=params(),
        cost_estimate=cost(count * height * 512 * 10, count * height * 512 * 12),
    )(wc, low, high, out)


def local(cov, wind_direction, wind_speed, speed_table, diffusivity):
    rows, tiles = cov.shape[0] // 128, cov.shape[1] // LANES
    n_row, n_col = lax.axis_size("row"), lax.axis_size("col")
    up = lambda n: [(i, i + 1) for i in range(n - 1)]
    down = lambda n: [(i + 1, i) for i in range(n - 1)]
    before = lax.ppermute(cov[-256:], "row", up(n_row))
    after = lax.ppermute(cov[:256], "row", down(n_row))
    wr, wc = weights_call(rows, tiles, wind_direction, wind_speed, speed_table, diffusivity)
    left, right = edge_call(cov, wr, 2, rows - 4)
    low = lax.ppermute(right, "col", up(n_col))
    high = lax.ppermute(left, "col", down(n_col))
    out = main_call(cov, wr, wc)
    top = jnp.concatenate([before, cov[:512]], axis=0)
    bottom = jnp.concatenate([cov[-512:], after], axis=0)
    tl, tr = edge_call(top, wr, 0, 2, inside=-2)
    bl, br = edge_call(bottom, wr, rows - 2, 2, inside=rows - 4)
    low_c = lax.ppermute(jnp.concatenate([tr, br]), "col", up(n_col))
    high_c = lax.ppermute(jnp.concatenate([tl, bl]), "col", down(n_col))
    out = rim_call(cov, wr, wc, before, after, out)
    out = halo_call(out, wc, low, high, (1, 1, rows // 2 - 2), 256)
    return halo_call(out, wc, low_c, high_c, (0, rows // 2 - 1, 2), 256)


def solution(mesh):
    return jax.shard_map(
        local,
        mesh=mesh,
        in_specs=(P("row", "col"), P(), P(), P(), P()),
        out_specs=P("row", "col"),
        check_vma=False,
    )
```

time: 844 us -> 297 us (0.35)
  other arithmetic: 384 us -> 10.5 us
  local copies, waits for them, and re-layouts: 322 us -> 9.85 us
  Pallas kernels: 0 us -> 218 us
  waiting for transfers between devices: 126 us -> 38.3 us
    add x4 -> x0, other arithmetic: 323 us -> none  [the longest x2 190 us: advance_flat(): weights[0] * middle + weights[1] * western + weights[2] * eastern]
    slice x16 -> x2, local copies, waits for them, and re-layouts: 319 us -> 8.25 us  [the longest x1 4.31 us: local(): top = jnp.concatenate([before, cov[:512]], axis=0)]
    pallas_call x0 -> x8, Pallas kernels: none -> 218 us  [the longest x1 108 us: main_call(): pl.pallas_call(functools.partial(main_kernel, wide // LANES), grid=(rows...]
    ppermute x4 -> x6, waiting for transfers between devices: 126 us -> 38.3 us  [the longest x1 38.3 us: local(): before = lax.ppermute(cov[-256:], 'row', up(n_row))]
    concatenate x2 -> x4, other arithmetic: 52.6 us -> 10.5 us  [the longest x1 5.09 us: local(): bottom = jnp.concatenate([cov[-512:], after], axis=0)]
    ppermute x4 -> x6, starting transfers between devices: 10.7 us -> 18.3 us  [the longest x1 5.3 us: local(): after = lax.ppermute(cov[:256], 'row', down(n_row))]
  transfers between devices with their start and end apart: 4 -> 6, of which waited for: 4 -> 1; matrix products, arithmetic and copies ran while one was open for 1% -> 6% of each run, Pallas kernels for 0% -> 57%
where the time goes in v1:
time: 297 us; the launch traced here: 295 us
  Pallas kernels  218 us (73%)
  waiting for transfers between devices  38.3 us (13%)
  starting transfers between devices  18.3 us (6%)
  other arithmetic  10.5 us (4%)
  local copies, waits for them, and re-layouts  9.85 us (3%)
    pallas_call x1, Pallas kernels, main_call(): pl.pallas_call(functools.partial(main_kernel, wide // LANES), grid=(rows...  108 us
    pallas_call x3, Pallas kernels, edge_call(): pl.pallas_call(functools.partial(edge_kernel, count, first), grid=(2,), i...  56.2 us
    ppermute x1, waiting for transfers between devices, local(): before = lax.ppermute(cov[-256:], 'row', up(n_row))  38.3 us
    pallas_call x2, Pallas kernels, halo_call(): pl.pallas_call(functools.partial(halo_kernel, wide // LANES), grid=(2, co...  33.1 us
    pallas_call x1, Pallas kernels, rim_call(): pl.pallas_call(functools.partial(rim_kernel, wide // LANES, rows), grid=(...  19.5 us
  transfers between devices with their start and end apart: 6, of which 1 were waited for; matrix products, arithmetic and copies ran while one was open for 6% of the time, Pallas kernels for 57%

profile of v1, /device:TPU:25, one launch (start us, length us, event | category | flops | bytes accessed | tf_op | source)
XLA Modules:
  0.0 295.4 jit_solution(12177397742961920526)
XLA Ops:
  0.0 2.1 shard_map.55
  2.1 43.9 %shard_map.58 = (f32[3584,256]{1,0:T(8,128)}, f32[3584,256]{1,0:T(8,128)}) custom-call(f32[5,128,128]{2,1,0:T(8,128)} %get-tuple-element.14.wr, f32[4096,2048]{1,0:T(8,128)} %c_ref.1, f32[4096,2048]{1,0:T(8,128)} %c_ref.1), custom_call_target="tpu_custom_call" | custom-call | flops 33030144 | bytes 14680064 | tf_op jit(solution)/shard_map/pallas_call | solution.py:152
  46.0 3.7 %collective-permute-start.4 = (f32[3584,256]{1,0:T(8,128)}, f32[3584,256]{1,0:T(8,128)}, u32[]{:S(2)}, u32[]{:S(2)}) collective-permute-start(f32[3584,256]{1,0:T(8,128)} %get-tuple-element.19), channel_id=1, source_target_pairs={{0,1},{1,2},{2,3},{3,4},{4,5},{5,6},{6,7},{8,9},{9,10},{10,11},{11... | collective-permute-start | bytes 11010056 | tf_op jit(solution)/shard_map/ppermute | solution.py:371
  49.7 2.5 collective-permute-start.5
  52.2 3.9 %fusion = (f32[256,2048]{1,0:T(8,128)S(1)}, f32[256,2048]{1,0:T(8,128)}) fusion(f32[4096,2048]{1,0:T(8,128)} %c_ref.1), kind=kLoop, calls=%fused_computation.4 | loop fusion | bytes 8388608 | tf_op jit(solution)/shard_map/slice | solution.py:367
  56.2 1.3 collective-permute-start
  57.5 5.3 %collective-permute-start.1 = (f32[256,2048]{1,0:T(8,128)}, f32[256,2048]{1,0:T(8,128)}, u32[]{:S(2)}, u32[]{:S(2)}) collective-permute-start(f32[256,2048]{1,0:T(8,128)} %get-tuple-element.22), channel_id=1, source_target_pairs={{8,0},{16,8},{24,16},{9,1},{17,9},{25,17},{10,2},{18,10},{26,18},{... | collective-permute-start | bytes 6291464 | tf_op jit(solution)/shard_map/ppermute | solution.py:368
  62.8 4.3 %fusion.1 = (f32[512,2048]{1,0:T(8,128)S(1)}, f32[512,2048]{1,0:T(8,128)S(1)}) fusion(f32[4096,2048]{1,0:T(8,128)} %c_ref.1), kind=kLoop, calls=%fused_computation.5 | loop fusion | bytes 16777216 | tf_op jit(solution)/shard_map/slice | solution.py:374
  67.1 38.3 %collective-permute-done.before = f32[256,2048]{1,0:T(8,128)S(1)} collective-permute-done((f32[256,2048]{1,0:T(8,128)S(1)}, f32[256,2048]{1,0:T(8,128)S(1)}, u32[]{:S(2)}, u32[]{:S(2)}) %collective-permute-start) | collective-permute-done | bytes 2097184 | tf_op jit(solution)/shard_map/ppermute | solution.py:367
  105.4 0.0 copy-start
  105.4 3.4 %pad_maximum_fusion.a.b = f32[768,2048]{1,0:T(8,128)} fusion(f32[512,2048]{1,0:T(8,128)S(1)} %get-tuple-element.23, f32[256,2048]{1,0:T(8,128)S(1)} %collective-permute-done.before), kind=kLoop, calls=%fused_computation | loop fusion | flops 1572864 | bytes 12582912 | tf_op jit(solution)/shard_map/concatenate | solution.py:374
  108.8 0.0 copy-done
  108.8 6.1 %shard_map.56 = (f32[256,256]{1,0:T(8,128)}, f32[256,256]{1,0:T(8,128)}) custom-call(f32[5,128,128]{2,1,0:T(8,128)} %get-tuple-element.14.wr, f32[768,2048]{1,0:T(8,128)} %pad_maximum_fusion.a.b, f32[768,2048]{1,0:T(8,128)} %pad_maximum_fusion.a.b), custom_call_target="tpu_custom_call" | custom-call | flops 2359296 | bytes 1048576 | tf_op jit(solution)/shard_map/pallas_call | solution.py:152
  114.9 0.0 collective-permute-done.1.after
  114.9 5.1 %pad_maximum_fusion.1.a.b = f32[768,2048]{1,0:T(8,128)} fusion(f32[256,2048]{1,0:T(8,128)} %collective-permute-done.1.after, f32[512,2048]{1,0:T(8,128)S(1)} %get-tuple-element.24), kind=kLoop, calls=%fused_computation.1 | loop fusion | flops 1572864 | bytes 12582912 | tf_op jit(solution)/shard_map/concatenate | solution.py:375
  120.0 6.2 %shard_map.57 = (f32[256,256]{1,0:T(8,128)}, f32[256,256]{1,0:T(8,128)}) custom-call(f32[5,128,128]{2,1,0:T(8,128)} %get-tuple-element.14.wr, f32[768,2048]{1,0:T(8,128)} %pad_maximum_fusion.1.a.b, f32[768,2048]{1,0:T(8,128)} %pad_maximum_fusion.1.a.b), custom_call_target="tpu_custom_call" | custom-call | flops 2359296 | bytes 1048576 | tf_op jit(solution)/shard_map/pallas_call | solution.py:152
  126.2 0.0 copy-done.4
  126.2 1.0 pad_maximum_fusion.3
  127.2 2.3 collective-permute-start.3
  129.5 0.0 copy-done.3
  129.5 1.0 pad_maximum_fusion.2
  130.5 3.3 %collective-permute-start.2 = (f32[512,256]{1,0:T(8,128)S(1)}, f32[512,256]{1,0:T(8,128)S(1)}, u32[]{:S(2)}, u32[]{:S(2)}) collective-permute-start(f32[512,256]{1,0:T(8,128)S(1)} %pad_maximum_fusion.2), channel_id=1, source_target_pairs={{0,1},{1,2},{2,3},{3,4},{4,5},{5,6},{6,7},{8,9},{9,10},{10,11},{11... | collective-permute-start | bytes 1572872 | tf_op jit(solution)/shard_map/ppermute | solution.py:378
  133.7 107.5 %shard_map.59._ = f32[4096,2048]{1,0:T(8,128)} custom-call(f32[5,128,128]{2,1,0:T(8,128)} %get-tuple-element.14.wr, f32[10,24,128]{2,1,0:T(8,128)} %get-tuple-element.13.wc, f32[4096,2048]{1,0:T(8,128)} %c_ref.1), custom_call_target="tpu_custom_call" | custom-call | flops 301989888 | bytes 67108864 | tf_op jit(solution)/shard_map/pallas_call | solution.py:257
  241.2 19.5 %shard_map.60.o_in = f32[4096,2048]{1,0:T(8,128)} custom-call(f32[5,128,128]{2,1,0:T(8,128)} %get-tuple-element.14.wr, f32[10,24,128]{2,1,0:T(8,128)} %get-tuple-element.13.wc, f32[256,2048]{1,0:T(8,128)} %copy-done, f32[256,2048]{1,0:T(8,128)} %collective-permute-done.1.after, f32[4096,2048]{1,0:T(8,128)} %c_ref.1, ...), custom_call_target="tpu_custom_call", output_to_operand_aliasing={{}: (5, {})} | custom-call | flops 33554432 | bytes 8388608 | tf_op jit(solution)/shard_map/pallas_call | solution.py:291
  260.7 0.0 collective-permute-done.4.low
  260.7 0.0 collective-permute-done.5.high
  260.7 27.9 %shard_map.61.o_in = f32[4096,2048]{1,0:T(8,128)} custom-call(f32[10,24,128]{2,1,0:T(8,128)} %get-tuple-element.13.wc, f32[3584,256]{1,0:T(8,128)} %collective-permute-done.4.low, f32[3584,256]{1,0:T(8,128)} %collective-permute-done.5.high, f32[4096,2048]{1,0:T(8,128)} %shard_map.60.o_in), custom_call_target="tpu_custom_call", output_to_operand_aliasing={{}: (3, {})} | custom-call | flops 18350080 | bytes 22020096 | tf_op jit(solution)/shard_map/pallas_call | solution.py:345
  288.6 0.0 collective-permute-done.3.high
  288.6 0.0 collective-permute-done.2.low
  288.6 0.8 copy-done.1
  289.4 0.8 copy-done.2
  290.2 5.2 %shard_map.62 = f32[4096,2048]{1,0:T(8,128)} custom-call(f32[10,24,128]{2,1,0:T(8,128)} %get-tuple-element.13.wc, f32[512,256]{1,0:T(8,128)} %copy-done.2, f32[512,256]{1,0:T(8,128)} %copy-done.1, f32[4096,2048]{1,0:T(8,128)} %shard_map.61.o_in), custom_call_target="tpu_custom_call", output_to_operand_aliasing={{}: (3, {})} | custom-call | flops 2621440 | bytes 3145728 | tf_op jit(solution)/shard_map/pallas_call | solution.py:345
  (4 shorter events, 0.0 us)
Async XLA Ops:
  46.0 214.7 %collective-permute-start.4 = (f32[3584,256]{1,0:T(8,128)}, f32[3584,256]{1,0:T(8,128)}, u32[]{:S(2)}, u32[]{:S(2)}) collective-permute-start(f32[3584,256]{1,0:T(8,128)} %get-tuple-element.19), channel_id=1, source_target_pairs={{0,1},{1,2},{2,3},{3,4},{4,5},{5,6},{6,7},{8,9},{9,10},{10,11},{11... | collective-permute-start | bytes 11010056 | tf_op jit(solution)/shard_map/ppermute | solution.py:371
  49.7 211.0 %collective-permute-start.5 = (f32[3584,256]{1,0:T(8,128)}, f32[3584,256]{1,0:T(8,128)}, u32[]{:S(2)}, u32[]{:S(2)}) collective-permute-start(f32[3584,256]{1,0:T(8,128)} %get-tuple-element.20), channel_id=1, source_target_pairs={{1,0},{2,1},{3,2},{4,3},{5,4},{6,5},{7,6},{9,8},{10,9},{11,10},{12... | collective-permute-start | bytes 11010056 | tf_op jit(solution)/shard_map/ppermute | solution.py:372
  56.2 49.2 %collective-permute-start = (f32[256,2048]{1,0:T(8,128)S(1)}, f32[256,2048]{1,0:T(8,128)S(1)}, u32[]{:S(2)}, u32[]{:S(2)}) collective-permute-start(f32[256,2048]{1,0:T(8,128)S(1)} %get-tuple-element.21), channel_id=1, source_target_pairs={{0,8},{8,16},{16,24},{1,9},{9,17},{17,25},{2,10},{10,18},{18,26},{... | collective-permute-start | bytes 6291464 | tf_op jit(solution)/shard_map/ppermute | solution.py:367
  57.5 57.4 %collective-permute-start.1 = (f32[256,2048]{1,0:T(8,128)}, f32[256,2048]{1,0:T(8,128)}, u32[]{:S(2)}, u32[]{:S(2)}) collective-permute-start(f32[256,2048]{1,0:T(8,128)} %get-tuple-element.22), channel_id=1, source_target_pairs={{8,0},{16,8},{24,16},{9,1},{17,9},{25,17},{10,2},{18,10},{26,18},{... | collective-permute-start | bytes 6291464 | tf_op jit(solution)/shard_map/ppermute | solution.py:368
  105.4 3.4 %copy-start = (f32[256,2048]{1,0:T(8,128)}, f32[256,2048]{1,0:T(8,128)S(1)}, u32[]{:S(2)}) copy-start(f32[256,2048]{1,0:T(8,128)S(1)} %collective-permute-done.before) | copy-start | bytes 6291460
  120.0 6.2 %copy-start.4 = (f32[256,256]{1,0:T(8,128)S(1)}, f32[256,256]{1,0:T(8,128)}, u32[]{:S(2)}) copy-start(f32[256,256]{1,0:T(8,128)} %get-tuple-element.17) | copy-start | bytes 786436
  120.0 9.5 %copy-start.3 = (f32[256,256]{1,0:T(8,128)S(1)}, f32[256,256]{1,0:T(8,128)}, u32[]{:S(2)}) copy-start(f32[256,256]{1,0:T(8,128)} %get-tuple-element.15) | copy-start | bytes 786436
  127.2 161.5 %collective-permute-start.3 = (f32[512,256]{1,0:T(8,128)S(1)}, f32[512,256]{1,0:T(8,128)S(1)}, u32[]{:S(2)}, u32[]{:S(2)}) collective-permute-start(f32[512,256]{1,0:T(8,128)S(1)} %pad_maximum_fusion.3), channel_id=1, source_target_pairs={{1,0},{2,1},{3,2},{4,3},{5,4},{6,5},{7,6},{9,8},{10,9},{11,10},{12... | collective-permute-start | bytes 1572872 | tf_op jit(solution)/shard_map/ppermute | solution.py:379
  130.5 158.2 %collective-permute-start.2 = (f32[512,256]{1,0:T(8,128)S(1)}, f32[512,256]{1,0:T(8,128)S(1)}, u32[]{:S(2)}, u32[]{:S(2)}) collective-permute-start(f32[512,256]{1,0:T(8,128)S(1)} %pad_maximum_fusion.2), channel_id=1, source_target_pairs={{0,1},{1,2},{2,3},{3,4},{4,5},{5,6},{6,7},{8,9},{9,10},{10,11},{11... | collective-permute-start | bytes 1572872 | tf_op jit(solution)/shard_map/ppermute | solution.py:378
  288.6 0.8 copy-start.1
  289.4 0.8 copy-start.2

commit v2 on v1

v2 whole, which is shorter than its diff:
```python
import functools

import jax
import jax.numpy as jnp
from jax import lax
from jax.experimental import pallas as pl
from jax.experimental.pallas import tpu as pltpu
from jax.sharding import PartitionSpec as P

NLAT = 128
NLON = 128
LANES = 128
PAD = 8
GROUPS = 2
F32 = jnp.float32
ANY = pl.BlockSpec(memory_space=pl.ANY)


def params(mib=56):
    return pltpu.CompilerParams(vmem_limit_bytes=mib << 20)


def cost(flops, size):
    return pl.CostEstimate(flops=flops, bytes_accessed=size, transcendentals=0)


def weights_kernel(rows, cols, wd, ws, table, diff, wr, kr, wc, s_wd, s_ws, s_k, tile):
    def parts(first, count, sub):
        for i in range(count):
            lat = jnp.clip(first + i, 0, NLAT - 1)
            at = pl.ds(pl.multiple_of(lat * NLON, NLON), NLON)
            s_wd[i : i + 1, :] = wd[sub : sub + 1, at]
            s_ws[i : i + 1, :] = ws[sub : sub + 1, at]
            s_k[i : i + 1, :] = jnp.full((1, LANES), diff[lat], F32)
        size = -(-count // 8) * 8
        speed, way, k = s_ws[:size, :], s_wd[:size, :], s_k[:size, :]
        u = v = jnp.zeros((size, LANES), F32)
        for c in range(table.shape[1]):
            u = jnp.where(speed == c, table[0, c], u)
            v = jnp.where(speed == c, table[1, c], v)
        lat = first + lax.broadcasted_iota(jnp.int32, (size, LANES), 0)
        keep = jnp.logical_and(lat >= 0, lat < NLAT)
        u, v, k = (jnp.where(keep, x, 0.0) for x in (u, v, k))
        whole = jnp.where(keep, 1.0 - 4.0 * k, 0.0)
        return jnp.where((way & 1) == 0, u, -u), jnp.where(way < 2, v, -v), k, whole

    lat_row = lax.axis_index("row") * rows
    lat_col = lax.axis_index("col") * cols
    count = rows + 5
    x0, y0, _, _ = parts(lat_row - 3, count, 0)
    x1, y1, k, whole = parts(lat_row - 4, count, 1)
    kr[0, : k.shape[0], :] = k
    kr[1, : k.shape[0], :] = whole
    tile[...] = jnp.zeros_like(tile)
    for g in range(wr.shape[0]):
        n = min(32, k.shape[0] - 32 * g)
        for a, x in enumerate((x0, y0, x1, y1)):
            tile[32 * a : 32 * a + n, :] = x[32 * g : 32 * g + n, :]
        wr[g] = tile[...].T
    for sub in range(2):
        x, y, k, whole = parts(lat_col - 1, cols + 2, sub)
        for a, o in enumerate(five(x, y, k, whole)):
            wc[5 * sub + a, : o.shape[0], :] = o


def five(x, y, k, whole):
    none = jnp.zeros_like(x)
    return (
        whole - jnp.abs(x) - jnp.abs(y),
        jnp.maximum(x, none) + k,
        k - jnp.minimum(x, none),
        jnp.maximum(y, none) + k,
        k - jnp.minimum(y, none),
    )


def weights_call(rows, cols, wd, ws, table, diff):
    most = -(-(max(rows, cols) + 5) // 8) * 8
    groups = -(-(rows + 4) // 32)
    smem = pl.BlockSpec(memory_space=pltpu.SMEM)
    vmem = pl.BlockSpec(memory_space=pltpu.VMEM)
    return pl.pallas_call(
        functools.partial(weights_kernel, rows, cols),
        in_specs=[vmem, vmem, smem, smem],
        out_specs=[vmem, vmem, vmem],
        out_shape=[
            jax.ShapeDtypeStruct((groups, NLON, LANES), F32),
            jax.ShapeDtypeStruct((2, -(-(rows + 5) // 8) * 8, LANES), F32),
            jax.ShapeDtypeStruct((10, -(-(cols + 2) // 8) * 8, LANES), F32),
        ],
        scratch_shapes=[
            pltpu.VMEM((most, LANES), jnp.int32),
            pltpu.VMEM((most, LANES), jnp.int32),
            pltpu.VMEM((most, LANES), F32),
            pltpu.VMEM((LANES, LANES), F32),
        ],
        compiler_params=params(),
        cost_estimate=cost(100000, 1 << 23),
    )(wd, ws, table, diff)


def lane_weights(wr, kr, index, row, sub, height=8):
    w = wr[index // 32, pl.ds(row, height), :]
    if isinstance(index, int):
        lane = [32 * (2 * sub + a) + index % 32 for a in range(2)]
    else:
        w = pltpu.roll(w, LANES - lax.rem(index, 32), 1)
        lane = [32 * (2 * sub + a) for a in range(2)]
    x, y = (jnp.broadcast_to(w[:, a : a + 1], (height, LANES)) for a in lane)
    k, whole = (jnp.broadcast_to(kr[a, pl.ds(index + 1 - sub, 1), :], (height, LANES)) for a in range(2))
    return five(x, y, k, whole)


def lay_out(wr, kr, index, row, W, subs=(0, 1)):
    for sub in subs:
        for k, x in enumerate(lane_weights(wr, kr, index, row, sub)):
            W[5 * sub + k, pl.ds(row, 8), :] = x


def edge_kernel(pieces, runs, n_refs, wr, kr, *refs):
    sources, (left, right), f, g, W, sem = refs[:n_refs], refs[n_refs : n_refs + 2], refs[-11:-7], refs[-7:-3], refs[-3:-1], refs[-1]
    sub_row = lax.broadcasted_iota(jnp.int32, (8, LANES), 0)
    wide = sources[0].shape[1]
    copies = []
    for i, (ref, row, count, place) in enumerate(pieces):
        for c, lane in enumerate((0, LANES, wide - 2 * LANES, wide - LANES)):
            copies.append(
                pltpu.make_async_copy(
                    sources[ref].at[pl.ds(row, count * 128), pl.ds(lane, LANES)],
                    f[c].at[pl.ds(place * 128, count * 128), :],
                    sem.at[4 * i + c],
                )
            )
    for c in copies:
        c.start()
    for c in copies:
        c.wait()

    def around(load, j):
        mid = load(8 * j)
        if j == 0:
            west = jnp.where(sub_row == 0, pltpu.roll(load(120), 1, 0), pltpu.roll(mid, 1, 0))
        else:
            west = load(8 * j - 1)
        if j == 15:
            east = jnp.where(sub_row == 7, pltpu.roll(load(0), 7, 0), pltpu.roll(mid, 7, 0))
        else:
            east = load(8 * j + 1)
        return mid, west, east

    def apply(src, base, index, sub, par, store):
        for j in range(16):
            lay_out(wr, kr, index + 1, 8 * j, W[1 - par], (sub,))
            w = [W[par][5 * sub + k, 8 * j : 8 * j + 8, :] for k in range(5)]
            for c in range(4):
                mid, west, east = around(lambda r: src[c][pl.ds(base + 128 + r, 8), :], j)
                so, no = src[c][pl.ds(base + 8 * j, 8), :], src[c][pl.ds(base + 256 + 8 * j, 8), :]
                store(c, 8 * j, w[0] * mid + w[1] * west + w[2] * east + w[3] * so + w[4] * no)

    def to_g(base, place, first, i, par):
        def store(c, r, x):
            g[c][pl.ds(base + r, 8), :] = x

        apply(f, pl.multiple_of(place * 128 + i * 128, 128), first + i + 2, 0, par, store)

    def to_out(base, first, i, at, par):
        def store(c, r, x):
            out = (left, right)[c // 2]
            out[pl.ds(at + r, 8), (c % 2) * LANES : (c % 2 + 1) * LANES] = x

        apply(g, base, first + i + 4, 1, par, store)

    for place, at, first, count in runs:
        for j in range(16):
            lay_out(wr, kr, first + 2, 8 * j, W[0], (0,))
            lay_out(wr, kr, first + 4, 8 * j, W[0], (1,))

        @pl.loop(0, count // 2 + 1)
        def _(i):
            for par in range(2):
                to_g(pl.multiple_of((2 * i + par) * 128, 128), place, first, 2 * i + par, par)

        @pl.loop(0, count // 2)
        def _(i):
            for par in range(2):
                k = 2 * i + par
                to_out(pl.multiple_of(k * 128, 128), first, k, pl.multiple_of(at * 128 + k * 128, 128), par)


def edge_call(sources, wr, kr, pieces, runs, later=()):
    sources = [*sources, *later]
    size = max(p + c for _, _, c, p in pieces)
    count = sum(r[3] for r in runs)
    out = jax.ShapeDtypeStruct((count * 128, 2 * LANES), F32)
    vmem = pl.BlockSpec(memory_space=pltpu.VMEM)
    return pl.pallas_call(
        functools.partial(edge_kernel, pieces, runs, len(sources)),
        in_specs=[vmem, vmem] + [ANY] * len(sources),
        out_specs=[vmem, vmem],
        out_shape=[out, out],
        scratch_shapes=[pltpu.VMEM((size * 128, LANES), F32)] * 4
        + [pltpu.VMEM((max(r[3] for r in runs) * 128 + 256, LANES), F32)] * 4
        + [pltpu.VMEM((10, 128, LANES), F32)] * 2
        + [pltpu.SemaphoreType.DMA((4 * len(pieces),))],
        compiler_params=params(),
        cost_estimate=cost(count * 128 * 512 * 18, count * 128 * 512 * 8),
    )(wr, kr, *sources)


def roll(x, k):
    return pltpu.roll(x, k, 1)


def one_lat(tiles, slot, mode, index, f_ref, f_base, o_ref, o_base, wr, kr, wc, F, G, W):
    Fs, F1, F2 = F[slot], F[(slot - 1) % 4], F[(slot - 2) % 4]
    G1, G2, G3 = G[(slot - 1) % 4], G[(slot - 2) % 4], G[(slot - 3) % 4]
    here, after = W[slot % 2], W[(slot + 1) % 2]

    @pl.loop(0, 16 // GROUPS)
    def _(j):
        rs = [pl.multiple_of(j * 8 * GROUPS + 8 * i, 8) for i in range(GROUPS)]
        for r in rs:
            lay_out(wr, kr, index + 1, r, after)
        w0 = [[here[k, pl.ds(r, 8), :] for k in range(5)] for r in rs] if mode >= 1 else None
        w1 = [[here[5 + k, pl.ds(r, 8), :] for k in range(5)] for r in rs] if mode >= 2 else None

        def first(c):
            out = []
            for i, r in enumerate(rs):
                x = f_ref[pl.ds(f_base + r, 8), c * LANES : (c + 1) * LANES]
                Fs[c, pl.ds(PAD + r, 8), :] = x
                if mode >= 1:
                    w = w0[i]
                    g = (
                        w[0] * F1[c, pl.ds(PAD + r, 8), :]
                        + w[1] * F1[c, pl.ds(PAD - 1 + r, 8), :]
                        + w[2] * F1[c, pl.ds(PAD + 1 + r, 8), :]
                        + w[3] * F2[c, pl.ds(PAD + r, 8), :]
                        + w[4] * x
                    )
                    G1[c, pl.ds(PAD + r, 8), :] = g
                    out.append(g)
            return out

        def second(c):
            g = first(c)
            return [
                w[0] * G2[c, pl.ds(PAD + r, 8), :]
                + w[1] * G2[c, pl.ds(PAD - 1 + r, 8), :]
                + w[2] * G2[c, pl.ds(PAD + 1 + r, 8), :]
                + w[3] * G3[c, pl.ds(PAD + r, 8), :]
                + w[4] * g[i]
                for i, (r, w) in enumerate(zip(rs, w1))
            ]

        def across(sub, c, mid, so, no):
            W = [jnp.broadcast_to(wc[5 * sub + k, c + 1 : c + 2, :], (8, LANES)) for k in range(5)]
            out = []
            for i in range(GROUPS):
                t = None
                if mid is not None:
                    t = W[0] * mid[i] + W[1] * roll(mid[i], 1) + W[2] * roll(mid[i], LANES - 1)
                if so is not None:
                    t = W[3] * so[i] if t is None else t + W[3] * so[i]
                if no is not None:
                    t = W[4] * no[i] if t is None else t + W[4] * no[i]
                out.append(t)
            return out

        if mode < 2:
            for c in range(tiles):
                first(c)
            return
        h, u = {-2: None, -1: None}, {-2: None}
        for c in range(tiles + 2):
            h[c] = second(c) if c < tiles else None
            u[c - 1] = across(0, c - 1, h[c - 1], h[c - 2], h[c])
            if c >= 2:
                o = across(1, c - 2, u[c - 2], u[c - 3], u[c - 1])
                for i, r in enumerate(rs):
                    o_ref[pl.ds(o_base + r, 8), (c - 2) * LANES : (c - 1) * LANES] = o[i]

    for ring in (Fs, G1) if mode >= 1 else (Fs,):
        ring[:, PAD - 1 : PAD, :] = ring[:, PAD + 127 : PAD + 128, :]
        ring[:, PAD + 128 : PAD + 129, :] = ring[:, PAD : PAD + 1, :]


def main_kernel(tiles, wr, kr, wc, f_ref, o_ref, done, *ring):
    F, G, W = ring[:4], ring[4:8], ring[8:]
    t = pl.program_id(0)

    def four(modes):
        for q in range(4):
            one_lat(tiles, q, modes[q], 4 * t + q + 2, f_ref, 128 * q, o_ref, 128 * q, wr, kr, wc, F, G, W)

    done[...] = jnp.zeros_like(done)
    pl.when(t == 0)(lambda: four((0, 0, 1, 1)))
    pl.when(t > 0)(lambda: four((2, 2, 2, 2)))


def rings(tiles):
    return [pltpu.VMEM((tiles, 128 + 2 * PAD, LANES), F32)] * 8 + [pltpu.VMEM((10, 128, LANES), F32)] * 2


def main_call(cov, wr, kr, wc):
    rows, wide = cov.shape[0] // 128, cov.shape[1]
    return pl.pallas_call(
        functools.partial(main_kernel, wide // LANES),
        grid=(rows // 4,),
        in_specs=[
            *[pl.BlockSpec(w.shape, lambda s: (0, 0, 0)) for w in (wr, kr, wc)],
            pl.BlockSpec((512, wide), lambda s: (s, 0)),
        ],
        out_specs=[
            pl.BlockSpec((pl.Element(512), pl.Element(wide)), lambda s: (128 * jnp.maximum(4 * s - 2, 2), 0)),
            pl.BlockSpec((8, LANES), lambda s: (0, 0)),
        ],
        out_shape=[jax.ShapeDtypeStruct(cov.shape, F32), jax.ShapeDtypeStruct((8, LANES), F32)],
        scratch_shapes=rings(wide // LANES),
        compiler_params=params(),
        cost_estimate=cost(cov.size * 36, cov.size * 8),
    )(wr, kr, wc, cov)


def rim_kernel(tiles, rows, wr, kr, wc, before, after, c_ref, _, o_ref, *ring):
    F, G, W = ring[:4], ring[4:8], ring[8:]
    side = pl.program_id(0)

    def six(refs, index):
        for q, (mode, (ref, base)) in enumerate(zip((0, 0, 1, 1, 2, 2), refs)):
            one_lat(tiles, q % 4, mode, index + q, ref, base, o_ref, 128 * (q - 4), wr, kr, wc, F, G, W)

    own = [(c_ref, 128 * q) for q in range(4)]
    pl.when(side == 0)(lambda: six([(before, 0), (before, 128)] + own, 0))
    pl.when(side == 1)(lambda: six(own + [(after, 0), (after, 128)], rows - 2))


def rim_call(cov, wr, kr, wc, before, after, out):
    rows, wide = cov.shape[0] // 128, cov.shape[1]
    halo = pl.BlockSpec((256, wide), lambda s: (0, 0))
    return pl.pallas_call(
        functools.partial(rim_kernel, wide // LANES, rows),
        grid=(2,),
        in_specs=[
            *[pl.BlockSpec(w.shape, lambda s: (0, 0, 0)) for w in (wr, kr, wc)],
            halo,
            halo,
            pl.BlockSpec((512, wide), lambda s: (s * (rows // 4 - 1), 0)),
            ANY,
        ],
        out_specs=pl.BlockSpec((256, wide), lambda s: (s * (rows // 2 - 1), 0)),
        out_shape=jax.ShapeDtypeStruct(cov.shape, F32),
        scratch_shapes=rings(wide // LANES),
        input_output_aliases={6: 0},
        compiler_params=params(),
        cost_estimate=cost(cov.size * 4, cov.size),
    )(wr, kr, wc, before, after, cov, out)


def halo_kernel(tiles, wc, low, high, o_in, o_ref):
    side = pl.program_id(0)
    height = o_ref.shape[0]

    def weight(sub, k, lat):
        return jnp.broadcast_to(wc[5 * sub + k, lat + 1 : lat + 2, :], (8, LANES))

    def add(ref, near, far, outer, edge, inner, way, at_edge, at_inner):
        a = [weight(0, k, outer) for k in (0, 1, 2, way)]
        b = weight(0, way, edge)
        d = [weight(1, k, edge) for k in (0, 1, 2, way)]
        e = weight(1, way, inner)

        @pl.loop(0, height // 128)
        def _(i):
            for j in range(16):
                at = pl.ds(pl.multiple_of(i * 128 + 8 * j, 8), 8)
                f1, f2 = ref[at, near : near + LANES], ref[at, far : far + LANES]
                u1 = a[0] * f1 + a[1] * roll(f1, 1) + a[2] * roll(f1, LANES - 1) + a[3] * f2
                u0 = b * f1
                o_ref[at, at_edge : at_edge + LANES] = o_in[at, at_edge : at_edge + LANES] + (
                    d[0] * u0 + d[1] * roll(u0, 1) + d[2] * roll(u0, LANES - 1) + d[3] * u1
                )
                o_ref[at, at_inner : at_inner + LANES] = o_in[at, at_inner : at_inner + LANES] + e * u0

    pl.when(side == 0)(lambda: add(low, LANES, 0, -1, 0, 1, 3, 0, LANES))
    pl.when(side == 1)(lambda: add(high, 0, LANES, tiles, tiles - 1, tiles - 2, 4, LANES, 0))


def halo_call(out, wc, low, high, blocks, first, step=None):
    wide = out.shape[1]
    height, count = blocks
    step = step or height
    at = pl.BlockSpec(
        (pl.Element(height), pl.Element(256)), lambda s, i: (128 * (first // 128 + step // 128 * i), 256 * (s * (wide // 256 - 1)))
    )
    return pl.pallas_call(
        functools.partial(halo_kernel, wide // LANES),
        grid=(2, count),
        in_specs=[
            pl.BlockSpec(wc.shape, lambda s, i: (0, 0, 0)),
            pl.BlockSpec((height, 256), lambda s, i: (jnp.where(s == 0, i, count - 1), 0)),
            pl.BlockSpec((height, 256), lambda s, i: (jnp.where(s == 1, i, 0), 0)),
            at,
        ],
        out_specs=at,
        out_shape=jax.ShapeDtypeStruct(out.shape, F32),
        input_output_aliases={3: 0},
        compiler_params=params(),
        cost_estimate=cost(count * height * 512 * 10, count * height * 512 * 12),
    )(wc, low, high, out)


def local(cov, wind_direction, wind_speed, speed_table, diffusivity):
    rows, tiles = cov.shape[0] // 128, cov.shape[1] // LANES
    n_row, n_col = lax.axis_size("row"), lax.axis_size("col")
    up = lambda n: [(i, i + 1) for i in range(n - 1)]
    down = lambda n: [(i + 1, i) for i in range(n - 1)]
    wr, kr, wc = weights_call(rows, tiles, wind_direction, wind_speed, speed_table, diffusivity)
    left, right = edge_call([cov], wr, kr, [(0, 0, rows, 0)], [(0, 0, 2, rows - 4)])
    before = lax.ppermute(cov[-256:], "row", up(n_row))
    after = lax.ppermute(cov[:256], "row", down(n_row))
    low = lax.ppermute(right, "col", up(n_col))
    high = lax.ppermute(left, "col", down(n_col))
    out, done = main_call(cov, wr, kr, wc)
    left, right = edge_call(
        [before, cov, after],
        wr,
        kr,
        [(0, 0, 2, 0), (1, 0, 4, 2), (1, 128 * (rows - 4), 4, 6), (2, 0, 2, 10)],
        [(0, 0, 0, 2), (6, 2, rows - 2, 2)],
        [done],
    )
    low_c = lax.ppermute(right, "col", up(n_col))
    high_c = lax.ppermute(left, "col", down(n_col))
    out = rim_call(cov, wr, kr, wc, before, after, out)
    out = halo_call(out, wc, low, high, (128 * (rows - 4) // 2, 2), 256)
    return halo_call(out, wc, low_c, high_c, (256, 2), 0, 128 * (rows - 2))


def solution(mesh):
    return jax.shard_map(
        local,
        mesh=mesh,
        in_specs=(P("row", "col"), P(), P(), P(), P()),
        out_specs=P("row", "col"),
        check_vma=False,
    )
```

time: 297 us -> 168 us (0.57)
  Pallas kernels: 218 us -> 139 us
  waiting for transfers between devices: 38.3 us -> 0.02 us
  other arithmetic: 10.5 us -> 0 us
    ppermute x1, waiting for transfers between devices: 38.3 us -> 0.01 us  [local(): before = lax.ppermute(cov[-256:], 'row', up(n_row))]
    pallas_call x1, Pallas kernels: 108 us -> 74.3 us  [main_call(): pl.pallas_call(functools.partial(main_kernel, wide // LANES), grid=(rows...]
    pallas_call x3 -> x2, Pallas kernels: 56.2 us -> 26.3 us  [edge_call(): pl.pallas_call(functools.partial(edge_kernel, pieces, runs, len(sources))...]
    pallas_call x2, Pallas kernels: 33.1 us -> 16.8 us  [halo_call(): pl.pallas_call(functools.partial(halo_kernel, wide // LANES), grid=(2, co...]
    concatenate x4 -> x0, other arithmetic: 10.5 us -> none  [the longest x1 5.09 us: local(): bottom = jnp.concatenate([cov[-512:], after], axis=0)]
    unnamed x10, local copies, waits for them, and re-layouts: 1.59 us -> 5.49 us
    slice x2 -> x1, local copies, waits for them, and re-layouts: 8.25 us -> 4.76 us  [local(): after = lax.ppermute(cov[:256], 'row', down(n_row))]
  transfers between devices with their start and end apart: 6 -> 6, of which waited for: 1 -> 0; matrix products, arithmetic and copies ran while one was open for 6% -> 3% of each run, Pallas kernels for 57% -> 68%
where the time goes in v2:
time: 168 us; the launch traced here: 166 us
  Pallas kernels  139 us (83%)
  starting transfers between devices  17.1 us (10%)
  local copies, waits for them, and re-layouts  10.2 us (6%)
    pallas_call x1, Pallas kernels, main_call(): pl.pallas_call(functools.partial(main_kernel, wide // LANES), grid=(rows...  74.3 us
    pallas_call x2, Pallas kernels, edge_call(): pl.pallas_call(functools.partial(edge_kernel, pieces, runs, len(sources))...  26.3 us
    pallas_call x1, Pallas kernels, rim_call(): pl.pallas_call(functools.partial(rim_kernel, wide // LANES, rows), grid=(...  19.3 us
    pallas_call x2, Pallas kernels, halo_call(): pl.pallas_call(functools.partial(halo_kernel, wide // LANES), grid=(2, co...  16.8 us
    unnamed x10, local copies, waits for them, and re-layouts  5.49 us
    slice x1, local copies, waits for them, and re-layouts, local(): after = lax.ppermute(cov[:256], 'row', down(n_row))  4.76 us
    ppermute x1, starting transfers between devices, local(): low_c = lax.ppermute(right, 'col', up(n_col))  4.2 us
    ppermute x1, starting transfers between devices, local(): after = lax.ppermute(cov[:256], 'row', down(n_row))  4.12 us
  transfers between devices with their start and end apart: 6, of which 0 were waited for; matrix products, arithmetic and copies ran while one was open for 3% of the time, Pallas kernels for 68%

profile of v2, /device:TPU:25, one launch (start us, length us, event | category | flops | bytes accessed | tf_op | source)
XLA Modules:
  0.0 166.2 jit_solution(14552162047377701790)
XLA Ops:
  0.0 2.0 %shard_map.55 = (f32[2,128,128]{2,1,0:T(8,128)}, f32[2,40,128]{2,1,0:T(8,128)}, f32[10,24,128]{2,1,0:T(8,128)}) custom-call(s32[2,16384]{1,0:T(2,128)} %wd.1, s32[2,16384]{1,0:T(2,128)} %ws.1, f32[2,8]{1,0:T(2,128)} %table.1, f32[128]{0:T(128)} %diff.1), custom_call_target="tpu_custom_call" | custom-call | flops 100000 | bytes 8388608 | tf_op jit(solution)/shard_map/pallas_call | solution.py:82
  2.0 19.1 %shard_map.58 = (f32[3584,256]{1,0:T(8,128)}, f32[3584,256]{1,0:T(8,128)}) custom-call(f32[2,128,128]{2,1,0:T(8,128)} %get-tuple-element.15.wr, f32[2,40,128]{2,1,0:T(8,128)} %get-tuple-element.16.kr, f32[4096,2048]{1,0:T(8,128)} %c_ref.1), custom_call_target="tpu_custom_call" | custom-call | flops 33030144 | bytes 14680064 | tf_op jit(solution)/shard_map/pallas_call | solution.py:196
  21.2 3.7 %collective-permute-start.4 = (f32[3584,256]{1,0:T(8,128)}, f32[3584,256]{1,0:T(8,128)S(1)}, u32[]{:S(2)}, u32[]{:S(2)}) collective-permute-start(f32[3584,256]{1,0:T(8,128)} %get-tuple-element.20), channel_id=1, source_target_pairs={{0,1},{1,2},{2,3},{3,4},{4,5},{5,6},{6,7},{8,9},{9,10},{10,11},{11... | collective-permute-start | bytes 11010056 | tf_op jit(solution)/shard_map/ppermute | solution.py:422
  24.8 1.9 %collective-permute-start.5 = (f32[3584,256]{1,0:T(8,128)}, f32[3584,256]{1,0:T(8,128)}, u32[]{:S(2)}, u32[]{:S(2)}) collective-permute-start(f32[3584,256]{1,0:T(8,128)} %get-tuple-element.21), channel_id=1, source_target_pairs={{1,0},{2,1},{3,2},{4,3},{5,4},{6,5},{7,6},{9,8},{10,9},{11,10},{12... | collective-permute-start | bytes 11010056 | tf_op jit(solution)/shard_map/ppermute | solution.py:423
  26.8 4.8 %fusion = (f32[256,2048]{1,0:T(8,128)}, f32[256,2048]{1,0:T(8,128)}) fusion(f32[4096,2048]{1,0:T(8,128)} %c_ref.1), kind=kLoop, calls=%fused_computation | loop fusion | bytes 8388608 | tf_op jit(solution)/shard_map/slice | solution.py:421
  31.5 1.3 collective-permute-start
  32.8 4.1 %collective-permute-start.1 = (f32[256,2048]{1,0:T(8,128)}, f32[256,2048]{1,0:T(8,128)S(1)}, u32[]{:S(2)}, u32[]{:S(2)}) collective-permute-start(f32[256,2048]{1,0:T(8,128)} %get-tuple-element.23), channel_id=1, source_target_pairs={{8,0},{16,8},{24,16},{9,1},{17,9},{25,17},{10,2},{18,10},{26,18},{... | collective-permute-start | bytes 6291464 | tf_op jit(solution)/shard_map/ppermute | solution.py:421
  36.9 74.3 %shard_map.56 = (f32[4096,2048]{1,0:T(8,128)}, f32[8,128]{1,0:T(8,128)}) custom-call(f32[2,128,128]{2,1,0:T(8,128)} %get-tuple-element.15.wr, f32[2,40,128]{2,1,0:T(8,128)} %get-tuple-element.16.kr, f32[10,24,128]{2,1,0:T(8,128)} %get-tuple-element.14.wc, f32[4096,2048]{1,0:T(8,128)} %c_ref.1), custom_call_target="tpu_custom_call" | custom-call | flops 301989888 | bytes 67108864 | tf_op jit(solution)/shard_map/pallas_call | solution.py:307
  111.3 0.0 collective-permute-done.refs_0_.before
  111.3 0.0 copy-start
  111.3 0.0 collective-permute-done.1.refs_2_.after
  111.3 0.0 copy-start.1
  111.3 1.4 copy-done
  112.7 0.7 copy-done.1
  113.3 7.1 %shard_map.57 = (f32[512,256]{1,0:T(8,128)}, f32[512,256]{1,0:T(8,128)}) custom-call(f32[2,128,128]{2,1,0:T(8,128)} %get-tuple-element.15.wr, f32[2,40,128]{2,1,0:T(8,128)} %get-tuple-element.16.kr, f32[256,2048]{1,0:T(8,128)} %copy-done, f32[4096,2048]{1,0:T(8,128)} %c_ref.1, f32[256,2048]{1,0:T(8,128)} %copy-done.1, f32[8,128]{1,0:T(8,128)} %get-tuple-element.17.refs_3_), custom_call_target="tpu_custom_call" | custom-call | flops 4718592 | bytes 2097152 | tf_op jit(solution)/shard_map/pallas_call | solution.py:196
  120.5 4.2 %collective-permute-start.2 = (f32[512,256]{1,0:T(8,128)}, f32[512,256]{1,0:T(8,128)S(1)}, u32[]{:S(2)}, u32[]{:S(2)}) collective-permute-start(f32[512,256]{1,0:T(8,128)} %get-tuple-element.18), channel_id=1, source_target_pairs={{0,1},{1,2},{2,3},{3,4},{4,5},{5,6},{6,7},{8,9},{9,10},{10,11},{11... | collective-permute-start | bytes 1572872 | tf_op jit(solution)/shard_map/ppermute | solution.py:433
  124.7 1.9 %collective-permute-start.3 = (f32[512,256]{1,0:T(8,128)}, f32[512,256]{1,0:T(8,128)S(1)}, u32[]{:S(2)}, u32[]{:S(2)}) collective-permute-start(f32[512,256]{1,0:T(8,128)} %get-tuple-element.19), channel_id=1, source_target_pairs={{1,0},{2,1},{3,2},{4,3},{5,4},{6,5},{7,6},{9,8},{10,9},{11,10},{12... | collective-permute-start | bytes 1572872 | tf_op jit(solution)/shard_map/ppermute | solution.py:434
  126.6 19.3 %shard_map.59.o_in = f32[4096,2048]{1,0:T(8,128)} custom-call(f32[2,128,128]{2,1,0:T(8,128)} %get-tuple-element.15.wr, f32[2,40,128]{2,1,0:T(8,128)} %get-tuple-element.16.kr, f32[10,24,128]{2,1,0:T(8,128)} %get-tuple-element.14.wc, f32[256,2048]{1,0:T(8,128)} %copy-done, f32[256,2048]{1,0:T(8,128)} %copy-done.1, ...), custom_call_target="tpu_custom_call", output_to_operand_aliasing={{}: (6, {})} | custom-call | flops 33554432 | bytes 8388608 | tf_op jit(solution)/shard_map/pallas_call | solution.py:341
  146.0 0.0 collective-permute-done.4.low
  146.0 0.0 copy-start.2
  146.0 0.0 collective-permute-done.5.high
  146.0 1.9 %copy-done.2 = f32[3584,256]{1,0:T(8,128)} copy-done((f32[3584,256]{1,0:T(8,128)}, f32[3584,256]{1,0:T(8,128)S(1)}, u32[]{:S(2)}) %copy-start.2) | copy-done | bytes 3670040
  147.9 12.6 %shard_map.60.o_in = f32[4096,2048]{1,0:T(8,128)} custom-call(f32[10,24,128]{2,1,0:T(8,128)} %get-tuple-element.14.wc, f32[3584,256]{1,0:T(8,128)} %copy-done.2, f32[3584,256]{1,0:T(8,128)} %collective-permute-done.5.high, f32[4096,2048]{1,0:T(8,128)} %shard_map.59.o_in), custom_call_target="tpu_custom_call", output_to_operand_aliasing={{}: (3, {})} | custom-call | flops 18350080 | bytes 22020096 | tf_op jit(solution)/shard_map/pallas_call | solution.py:396
  160.5 0.0 collective-permute-done.2.low
  160.5 0.0 copy-start.3
  160.5 0.0 collective-permute-done.3.high
  160.5 0.8 copy-done.3
  161.3 0.0 copy-start.4
  161.3 0.8 copy-done.4
  162.1 4.2 %shard_map.61 = f32[4096,2048]{1,0:T(8,128)} custom-call(f32[10,24,128]{2,1,0:T(8,128)} %get-tuple-element.14.wc, f32[512,256]{1,0:T(8,128)} %copy-done.3, f32[512,256]{1,0:T(8,128)} %copy-done.4, f32[4096,2048]{1,0:T(8,128)} %shard_map.60.o_in), custom_call_target="tpu_custom_call", output_to_operand_aliasing={{}: (3, {})} | custom-call | flops 2621440 | bytes 3145728 | tf_op jit(solution)/shard_map/pallas_call | solution.py:396
Async XLA Ops:
  21.2 124.8 %collective-permute-start.4 = (f32[3584,256]{1,0:T(8,128)}, f32[3584,256]{1,0:T(8,128)S(1)}, u32[]{:S(2)}, u32[]{:S(2)}) collective-permute-start(f32[3584,256]{1,0:T(8,128)} %get-tuple-element.20), channel_id=1, source_target_pairs={{0,1},{1,2},{2,3},{3,4},{4,5},{5,6},{6,7},{8,9},{9,10},{10,11},{11... | collective-permute-start | bytes 11010056 | tf_op jit(solution)/shard_map/ppermute | solution.py:422
  24.8 121.1 %collective-permute-start.5 = (f32[3584,256]{1,0:T(8,128)}, f32[3584,256]{1,0:T(8,128)}, u32[]{:S(2)}, u32[]{:S(2)}) collective-permute-start(f32[3584,256]{1,0:T(8,128)} %get-tuple-element.21), channel_id=1, source_target_pairs={{1,0},{2,1},{3,2},{4,3},{5,4},{6,5},{7,6},{9,8},{10,9},{11,10},{12... | collective-permute-start | bytes 11010056 | tf_op jit(solution)/shard_map/ppermute | solution.py:423
  31.5 79.8 %collective-permute-start = (f32[256,2048]{1,0:T(8,128)}, f32[256,2048]{1,0:T(8,128)S(1)}, u32[]{:S(2)}, u32[]{:S(2)}) collective-permute-start(f32[256,2048]{1,0:T(8,128)} %get-tuple-element.24), channel_id=1, source_target_pairs={{0,8},{8,16},{16,24},{1,9},{9,17},{17,25},{2,10},{10,18},{18,26},{... | collective-permute-start | bytes 6291464 | tf_op jit(solution)/shard_map/ppermute | solution.py:420
  32.8 78.5 %collective-permute-start.1 = (f32[256,2048]{1,0:T(8,128)}, f32[256,2048]{1,0:T(8,128)S(1)}, u32[]{:S(2)}, u32[]{:S(2)}) collective-permute-start(f32[256,2048]{1,0:T(8,128)} %get-tuple-element.23), channel_id=1, source_target_pairs={{8,0},{16,8},{24,16},{9,1},{17,9},{25,17},{10,2},{18,10},{26,18},{... | collective-permute-start | bytes 6291464 | tf_op jit(solution)/shard_map/ppermute | solution.py:421
  111.3 1.4 copy-start
  111.3 2.0 %copy-start.1 = (f32[256,2048]{1,0:T(8,128)}, f32[256,2048]{1,0:T(8,128)S(1)}, u32[]{:S(2)}) copy-start(f32[256,2048]{1,0:T(8,128)S(1)} %collective-permute-done.1.refs_2_.after) | copy-start | bytes 6291460
  120.5 40.0 %collective-permute-start.2 = (f32[512,256]{1,0:T(8,128)}, f32[512,256]{1,0:T(8,128)S(1)}, u32[]{:S(2)}, u32[]{:S(2)}) collective-permute-start(f32[512,256]{1,0:T(8,128)} %get-tuple-element.18), channel_id=1, source_target_pairs={{0,1},{1,2},{2,3},{3,4},{4,5},{5,6},{6,7},{8,9},{9,10},{10,11},{11... | collective-permute-start | bytes 1572872 | tf_op jit(solution)/shard_map/ppermute | solution.py:433
  124.7 35.8 %collective-permute-start.3 = (f32[512,256]{1,0:T(8,128)}, f32[512,256]{1,0:T(8,128)S(1)}, u32[]{:S(2)}, u32[]{:S(2)}) collective-permute-start(f32[512,256]{1,0:T(8,128)} %get-tuple-element.19), channel_id=1, source_target_pairs={{1,0},{2,1},{3,2},{4,3},{5,4},{6,5},{7,6},{9,8},{10,9},{11,10},{12... | collective-permute-start | bytes 1572872 | tf_op jit(solution)/shard_map/ppermute | solution.py:434
  146.0 1.9 %copy-start.2 = (f32[3584,256]{1,0:T(8,128)}, f32[3584,256]{1,0:T(8,128)S(1)}, u32[]{:S(2)}) copy-start(f32[3584,256]{1,0:T(8,128)S(1)} %collective-permute-done.4.low) | copy-start | bytes 11010052
  160.5 0.8 copy-start.3
  161.3 0.8 copy-start.4

commit v3 on v2

--- a/solution.py
+++ b/solution.py
@@ -16,7 +16,7 @@
 ANY = pl.BlockSpec(memory_space=pl.ANY)
 
 
-def params(mib=56):
+def params(mib=63):
     return pltpu.CompilerParams(vmem_limit_bytes=mib << 20)
 
 
@@ -47,8 +47,9 @@
     lat_row = lax.axis_index("row") * rows
     lat_col = lax.axis_index("col") * cols
     count = rows + 5
-    x0, y0, _, _ = parts(lat_row - 3, count, 0)
-    x1, y1, k, whole = parts(lat_row - 4, count, 1)
+    x0, y0, _, _ = parts(lat_row - 4, count, 0)
+    x1, y1, _, _ = parts(lat_row - 5, count, 1)
+    _, _, k, whole = parts(lat_row - 4, count, 1)
     kr[0, : k.shape[0], :] = k
     kr[1, : k.shape[0], :] = whole
     tile[...] = jnp.zeros_like(tile)
@@ -76,7 +77,7 @@
 
 def weights_call(rows, cols, wd, ws, table, diff):
     most = -(-(max(rows, cols) + 5) // 8) * 8
-    groups = -(-(rows + 4) // 32)
+    groups = -(-(rows + 5) // 32)
     smem = pl.BlockSpec(memory_space=pltpu.SMEM)
     vmem = pl.BlockSpec(memory_space=pltpu.VMEM)
     return pl.pallas_call(
@@ -100,11 +101,11 @@
 
 
 def lane_weights(wr, kr, index, row, sub, height=8):
-    w = wr[index // 32, pl.ds(row, height), :]
+    w = wr[(index + 1) // 32, pl.ds(row, height), :]
     if isinstance(index, int):
-        lane = [32 * (2 * sub + a) + index % 32 for a in range(2)]
+        lane = [32 * (2 * sub + a) + (index + 1) % 32 for a in range(2)]
     else:
-        w = pltpu.roll(w, LANES - lax.rem(index, 32), 1)
+        w = pltpu.roll(w, LANES - lax.rem(index + 1, 32), 1)
         lane = [32 * (2 * sub + a) for a in range(2)]
     x, y = (jnp.broadcast_to(w[:, a : a + 1], (height, LANES)) for a in lane)
     k, whole = (jnp.broadcast_to(kr[a, pl.ds(index + 1 - sub, 1), :], (height, LANES)) for a in range(2))
@@ -117,8 +118,11 @@
             W[5 * sub + k, pl.ds(row, 8), :] = x
 
 
-def edge_kernel(pieces, runs, n_refs, wr, kr, *refs):
-    sources, (left, right), f, g, W, sem = refs[:n_refs], refs[n_refs : n_refs + 2], refs[-11:-7], refs[-7:-3], refs[-3:-1], refs[-1]
+def edge_kernel(pieces, runs, waits, n_refs, rims, wr, kr, *refs):
+    sources, to = refs[:n_refs], refs[n_refs : n_refs + 2]
+    if rims:
+        rim_to, rim_vmem, rim_sem, refs = refs[n_refs + 2 : n_refs + 4], refs[-3:-1], refs[-1], refs[:-3]
+    (left, right), f, g, W, sem, sent = refs[-14:-12], refs[-12:-8], refs[-8:-4], refs[-4:-2], refs[-2], refs[-1]
     sub_row = lax.broadcasted_iota(jnp.int32, (8, LANES), 0)
     wide = sources[0].shape[1]
     copies = []
@@ -133,8 +137,15 @@
             )
     for c in copies:
         c.start()
-    for c in copies:
-        c.wait()
+    if rims:
+        height = sources[0].shape[0]
+        rim_in = [
+            pltpu.make_async_copy(sources[0].at[pl.ds(at, 256), :], rim_vmem[i], rim_sem.at[i])
+            for i, at in enumerate((0, height - 256))
+        ]
+        rim_out = [pltpu.make_async_copy(rim_vmem[i], rim_to[i], rim_sem.at[2 + i]) for i in range(2)]
+        for c in rim_in:
+            c.start()
 
     def around(load, j):
         mid = load(8 * j)
@@ -170,48 +181,74 @@
 
         apply(g, base, first + i + 4, 1, par, store)
 
-    for place, at, first, count in runs:
+    out = []
+    for run, (place, at, first, count) in enumerate(runs):
         for j in range(16):
             lay_out(wr, kr, first + 2, 8 * j, W[0], (0,))
             lay_out(wr, kr, first + 4, 8 * j, W[0], (1,))
-
-        @pl.loop(0, count // 2 + 1)
-        def _(i):
-            for par in range(2):
-                to_g(pl.multiple_of((2 * i + par) * 128, 128), place, first, 2 * i + par, par)
-
-        @pl.loop(0, count // 2)
-        def _(i):
-            for par in range(2):
-                k = 2 * i + par
-                to_out(pl.multiple_of(k * 128, 128), first, k, pl.multiple_of(at * 128 + k * 128, 128), par)
-
-
-def edge_call(sources, wr, kr, pieces, runs, later=()):
-    sources = [*sources, *later]
+        done = 0
+        for chunk, size in enumerate(chunks(count)):
+            for p in waits[run][chunk]:
+                for c in copies[4 * p : 4 * p + 4]:
+                    c.wait()
+            g_first = done + 2 if done else 0
+
+            @pl.loop(g_first // 2, (done + size + 2) // 2)
+            def _(i):
+                for par in range(2):
+                    to_g(pl.multiple_of((2 * i + par) * 128, 128), place, first, 2 * i + par, par)
+
+            @pl.loop(done // 2, (done + size) // 2)
+            def _(i):
+                for par in range(2):
+                    k = 2 * i + par
+                    to_out(pl.multiple_of(k * 128, 128), first, k, pl.multiple_of(at * 128 + k * 128, 128), par)
+
+            rows = pl.ds((at + done) * 128, size * 128)
+            for i, (a, b) in enumerate(((left, to[0]), (right, to[1]))):
+                out.append(pltpu.make_async_copy(a.at[rows, :], b.at[rows, :], sent.at[len(out)]))
+                out[-1].start()
+            done += size
+            if rims and chunk == 0:
+                for c, d in zip(rim_in, rim_out):
+                    c.wait()
+                    d.start()
+    for c in out + (rim_out if rims else []):
+        c.wait()
+
+
+def chunks(count):
+    return [8] * (count // 8) + ([count % 8] if count % 8 else [])
+
+
+def edge_call(sources, wr, kr, pieces, runs, waits, later=(), rims=False):
     size = max(p + c for _, _, c, p in pieces)
     count = sum(r[3] for r in runs)
     out = jax.ShapeDtypeStruct((count * 128, 2 * LANES), F32)
     vmem = pl.BlockSpec(memory_space=pltpu.VMEM)
+    n = sum(len(chunks(r[3])) for r in runs)
+    rim = jax.ShapeDtypeStruct((256, sources[0].shape[1]), F32)
     return pl.pallas_call(
-        functools.partial(edge_kernel, pieces, runs, len(sources)),
-        in_specs=[vmem, vmem] + [ANY] * len(sources),
-        out_specs=[vmem, vmem],
-        out_shape=[out, out],
-        scratch_shapes=[pltpu.VMEM((size * 128, LANES), F32)] * 4
+        functools.partial(edge_kernel, pieces, runs, waits, len(sources) + len(later), rims),
+        in_specs=[vmem, vmem] + [vmem if x.shape[0] == 256 else ANY for x in sources] + [ANY] * len(later),
+        out_specs=[ANY] * (4 if rims else 2),
+        out_shape=[out, out] + ([rim, rim] if rims else []),
+        scratch_shapes=[pltpu.VMEM(out.shape, F32)] * 2
+        + [pltpu.VMEM((size * 128, LANES), F32)] * 4
         + [pltpu.VMEM((max(r[3] for r in runs) * 128 + 256, LANES), F32)] * 4
         + [pltpu.VMEM((10, 128, LANES), F32)] * 2
-        + [pltpu.SemaphoreType.DMA((4 * len(pieces),))],
+        + [pltpu.SemaphoreType.DMA((4 * len(pieces),)), pltpu.SemaphoreType.DMA((2 * n,))]
+        + ([pltpu.VMEM(rim.shape, F32)] * 2 + [pltpu.SemaphoreType.DMA((4,))] if rims else []),
         compiler_params=params(),
         cost_estimate=cost(count * 128 * 512 * 18, count * 128 * 512 * 8),
-    )(wr, kr, *sources)
+    )(wr, kr, *sources, *later)
 
 
 def roll(x, k):
     return pltpu.roll(x, k, 1)
 
 
-def one_lat(tiles, slot, mode, index, f_ref, f_base, o_ref, o_base, wr, kr, wc, F, G, W):
+def one_lat(tiles, slot, mode, index, f_ref, f_base, o_ref, o_base, next_weights, kr, wc, F, G, W):
     Fs, F1, F2 = F[slot], F[(slot - 1) % 4], F[(slot - 2) % 4]
     G1, G2, G3 = G[(slot - 1) % 4], G[(slot - 2) % 4], G[(slot - 3) % 4]
     here, after = W[slot % 2], W[(slot + 1) % 2]
@@ -220,9 +257,16 @@
     def _(j):
         rs = [pl.multiple_of(j * 8 * GROUPS + 8 * i, 8) for i in range(GROUPS)]
         for r in rs:
-            lay_out(wr, kr, index + 1, r, after)
-        w0 = [[here[k, pl.ds(r, 8), :] for k in range(5)] for r in rs] if mode >= 1 else None
-        w1 = [[here[5 + k, pl.ds(r, 8), :] for k in range(5)] for r in rs] if mode >= 2 else None
+            w, lane = next_weights(r)
+            for a in range(4):
+                after[a, pl.ds(r, 8), :] = jnp.broadcast_to(w[:, 32 * a + lane : 32 * a + lane + 1], (8, LANES))
+
+        def weights(sub):
+            k, whole = (jnp.broadcast_to(kr[a, pl.ds(index + 1 - sub, 1), :], (8, LANES)) for a in range(2))
+            return [five(here[2 * sub, pl.ds(r, 8), :], here[2 * sub + 1, pl.ds(r, 8), :], k, whole) for r in rs]
+
+        w0 = weights(0) if mode >= 1 else None
+        w1 = weights(1) if mode >= 2 else None
 
         def first(c):
             out = []
@@ -286,12 +330,14 @@
 
 
 def main_kernel(tiles, wr, kr, wc, f_ref, o_ref, done, *ring):
-    F, G, W = ring[:4], ring[4:8], ring[8:]
+    F, G, W, turned = ring[:4], ring[4:8], ring[8:10], ring[10]
     t = pl.program_id(0)
+    turned[...] = pltpu.roll(wr[(4 * t + 4) // 32], LANES - lax.rem(4 * t + 4, 32), 1)
 
     def four(modes):
         for q in range(4):
-            one_lat(tiles, q, modes[q], 4 * t + q + 2, f_ref, 128 * q, o_ref, 128 * q, wr, kr, wc, F, G, W)
+            next_weights = lambda r, q=q: (turned[pl.ds(r, 8), :], q)
+            one_lat(tiles, q, modes[q], 4 * t + q + 2, f_ref, 128 * q, o_ref, 128 * q, next_weights, kr, wc, F, G, W)
 
     done[...] = jnp.zeros_like(done)
     pl.when(t == 0)(lambda: four((0, 0, 1, 1)))
@@ -299,7 +345,7 @@
 
 
 def rings(tiles):
-    return [pltpu.VMEM((tiles, 128 + 2 * PAD, LANES), F32)] * 8 + [pltpu.VMEM((10, 128, LANES), F32)] * 2
+    return [pltpu.VMEM((tiles, 128 + 2 * PAD, LANES), F32)] * 8 + [pltpu.VMEM((4, 128, LANES), F32)] * 2
 
 
 def main_call(cov, wr, kr, wc):
@@ -316,97 +362,137 @@
             pl.BlockSpec((8, LANES), lambda s: (0, 0)),
         ],
         out_shape=[jax.ShapeDtypeStruct(cov.shape, F32), jax.ShapeDtypeStruct((8, LANES), F32)],
-        scratch_shapes=rings(wide // LANES),
+        scratch_shapes=rings(wide // LANES) + [pltpu.VMEM((128, LANES), F32)],
         compiler_params=params(),
         cost_estimate=cost(cov.size * 36, cov.size * 8),
     )(wr, kr, wc, cov)
 
 
-def rim_kernel(tiles, rows, wr, kr, wc, before, after, c_ref, _, o_ref, *ring):
-    F, G, W = ring[:4], ring[4:8], ring[8:]
-    side = pl.program_id(0)
-
-    def six(refs, index):
-        for q, (mode, (ref, base)) in enumerate(zip((0, 0, 1, 1, 2, 2), refs)):
-            one_lat(tiles, q % 4, mode, index + q, ref, base, o_ref, 128 * (q - 4), wr, kr, wc, F, G, W)
-
-    own = [(c_ref, 128 * q) for q in range(4)]
-    pl.when(side == 0)(lambda: six([(before, 0), (before, 128)] + own, 0))
-    pl.when(side == 1)(lambda: six(own + [(after, 0), (after, 128)], rows - 2))
-
-
-def rim_call(cov, wr, kr, wc, before, after, out):
-    rows, wide = cov.shape[0] // 128, cov.shape[1]
-    halo = pl.BlockSpec((256, wide), lambda s: (0, 0))
-    return pl.pallas_call(
-        functools.partial(rim_kernel, wide // LANES, rows),
-        grid=(2,),
-        in_specs=[
-            *[pl.BlockSpec(w.shape, lambda s: (0, 0, 0)) for w in (wr, kr, wc)],
-            halo,
-            halo,
-            pl.BlockSpec((512, wide), lambda s: (s * (rows // 4 - 1), 0)),
-            ANY,
-        ],
-        out_specs=pl.BlockSpec((256, wide), lambda s: (s * (rows // 2 - 1), 0)),
-        out_shape=jax.ShapeDtypeStruct(cov.shape, F32),
-        scratch_shapes=rings(wide // LANES),
-        input_output_aliases={6: 0},
-        compiler_params=params(),
-        cost_estimate=cost(cov.size * 4, cov.size),
-    )(wr, kr, wc, before, after, cov, out)
-
-
-def halo_kernel(tiles, wc, low, high, o_in, o_ref):
-    side = pl.program_id(0)
-    height = o_ref.shape[0]
+def add_halo(tiles, wc, side, halo, e_ref):
+    edge, way = (0, 3) if side == 0 else (tiles - 1, 4)
+    outer, inner = (-1, 1) if side == 0 else (tiles, tiles - 2)
+    near, far = (LANES, 0) if side == 0 else (0, LANES)
+    at_edge, at_inner = (0, LANES) if side == 0 else (LANES, 0)
 
     def weight(sub, k, lat):
         return jnp.broadcast_to(wc[5 * sub + k, lat + 1 : lat + 2, :], (8, LANES))
 
-    def add(ref, near, far, outer, edge, inner, way, at_edge, at_inner):
-        a = [weight(0, k, outer) for k in (0, 1, 2, way)]
-        b = weight(0, way, edge)
-        d = [weight(1, k, edge) for k in (0, 1, 2, way)]
-        e = weight(1, way, inner)
-
-        @pl.loop(0, height // 128)
-        def _(i):
-            for j in range(16):
-                at = pl.ds(pl.multiple_of(i * 128 + 8 * j, 8), 8)
-                f1, f2 = ref[at, near : near + LANES], ref[at, far : far + LANES]
-                u1 = a[0] * f1 + a[1] * roll(f1, 1) + a[2] * roll(f1, LANES - 1) + a[3] * f2
-                u0 = b * f1
-                o_ref[at, at_edge : at_edge + LANES] = o_in[at, at_edge : at_edge + LANES] + (
-                    d[0] * u0 + d[1] * roll(u0, 1) + d[2] * roll(u0, LANES - 1) + d[3] * u1
-                )
-                o_ref[at, at_inner : at_inner + LANES] = o_in[at, at_inner : at_inner + LANES] + e * u0
-
-    pl.when(side == 0)(lambda: add(low, LANES, 0, -1, 0, 1, 3, 0, LANES))
-    pl.when(side == 1)(lambda: add(high, 0, LANES, tiles, tiles - 1, tiles - 2, 4, LANES, 0))
-
-
-def halo_call(out, wc, low, high, blocks, first, step=None):
-    wide = out.shape[1]
-    height, count = blocks
-    step = step or height
-    at = pl.BlockSpec(
-        (pl.Element(height), pl.Element(256)), lambda s, i: (128 * (first // 128 + step // 128 * i), 256 * (s * (wide // 256 - 1)))
-    )
+    a = [weight(0, k, outer) for k in (0, 1, 2, way)]
+    b = weight(0, way, edge)
+    d = [weight(1, k, edge) for k in (0, 1, 2, way)]
+    e = weight(1, way, inner)
+
+    @pl.loop(0, halo.shape[0] // 128)
+    def _(i):
+        for j in range(16):
+            at = pl.ds(pl.multiple_of(i * 128 + 8 * j, 8), 8)
+            f1, f2 = halo[at, near : near + LANES], halo[at, far : far + LANES]
+            u1 = a[0] * f1 + a[1] * roll(f1, 1) + a[2] * roll(f1, LANES - 1) + a[3] * f2
+            u0 = b * f1
+            e_ref[at, at_edge : at_edge + LANES] = e_ref[at, at_edge : at_edge + LANES] + (
+                d[0] * u0 + d[1] * roll(u0, 1) + d[2] * roll(u0, LANES - 1) + d[3] * u1
+            )
+            e_ref[at, at_inner : at_inner + LANES] = e_ref[at, at_inner : at_inner + LANES] + e * u0
+
+
+class Copies:
+    def __init__(self, sem):
+        self.sem, self.n = sem, 0
+
+    def start(self, src, dst):
+        c = pltpu.make_async_copy(src, dst, self.sem.at[self.n])
+        self.n += 1
+        c.start()
+        return c
+
+
+def tail_kernel(tiles, rows, wr, kr, wc, before, after, low, high, cov, o_in, o_hbm, *scratch):
+    halo, own, rim, side_halo, side_own = (scratch[2 * i : 2 * i + 2] for i in range(5))
+    F, G, W, sem = scratch[10:14], scratch[14:18], scratch[18:20], scratch[20]
+    copies = Copies(sem)
+    wide, size = tiles * LANES, (rows - 4) * 128
+    inside = pl.ds(256, size)
+    lanes = [pl.ds(0, 256), pl.ds(wide - 256, 256)]
+
+    def bring(i):
+        if i < 2:
+            x = (before, after)[i]
+            return [copies.start(x, halo[i]), copies.start(cov.at[pl.ds(i * (rows - 4) * 128, 512), :], own[i])]
+        x = (low, high)[i - 2]
+        return [copies.start(x, side_halo[i - 2]), copies.start(o_in.at[inside, lanes[i - 2]], side_own[i - 2])]
+
+    ins, out = [bring(0)], []
+    for i in range(2):
+        for c in ins[i]:
+            c.wait()
+        ins += [bring(1), bring(2)] if i == 0 else [bring(3)]
+        mine, theirs = [(own[i], 128 * q) for q in range(4)], [(halo[i], 128 * q) for q in range(2)]
+        index = (rows - 2) * i
+        for q, (mode, (ref, base)) in enumerate(zip((0, 0, 1, 1, 2, 2), mine + theirs if i else theirs + mine)):
+            at = index + q + 2
+            next_weights = lambda r, at=at: (wr[at // 32, pl.ds(r, 8), :], at % 32)
+            one_lat(tiles, q % 4, mode, index + q, ref, base, rim[i], 128 * (q - 4), next_weights, kr, wc, F, G, W)
+        out.append(copies.start(rim[i], o_hbm.at[pl.ds(i * (rows - 2) * 128, 256), :]))
+    for i in range(2):
+        for c in ins[2 + i]:
+            c.wait()
+        add_halo(tiles, wc, i, side_halo[i], side_own[i])
+        out.append(copies.start(side_own[i], o_hbm.at[inside, lanes[i]]))
+    for c in out:
+        c.wait()
+
+
+def tail_call(cov, wr, kr, wc, before, after, low, high, out):
+    rows, wide = cov.shape[0] // 128, cov.shape[1]
+    vmem = pl.BlockSpec(memory_space=pltpu.VMEM)
     return pl.pallas_call(
-        functools.partial(halo_kernel, wide // LANES),
-        grid=(2, count),
-        in_specs=[
-            pl.BlockSpec(wc.shape, lambda s, i: (0, 0, 0)),
-            pl.BlockSpec((height, 256), lambda s, i: (jnp.where(s == 0, i, count - 1), 0)),
-            pl.BlockSpec((height, 256), lambda s, i: (jnp.where(s == 1, i, 0), 0)),
-            at,
-        ],
-        out_specs=at,
+        functools.partial(tail_kernel, wide // LANES, rows),
+        in_specs=[vmem] * 3 + [ANY] * 6,
+        out_specs=ANY,
+        out_shape=jax.ShapeDtypeStruct(cov.shape, F32),
+        scratch_shapes=[pltpu.VMEM((256, wide), F32)] * 2
+        + [pltpu.VMEM((512, wide), F32)] * 2
+        + [pltpu.VMEM((256, wide), F32)] * 2
+        + [pltpu.VMEM(low.shape, F32)] * 4
+        + rings(wide // LANES)
+        + [pltpu.SemaphoreType.DMA((12,))],
+        input_output_aliases={8: 0},
+        compiler_params=params(),
+        cost_estimate=cost(cov.size * 8, cov.size * 3),
+    )(wr, kr, wc, before, after, low, high, cov, out)
+
+
+def corner_kernel(tiles, rows, wc, low, high, o_in, o_hbm, own0, own1, halo0, halo1, sem):
+    copies = Copies(sem)
+    wide = tiles * LANES
+    parts = [(i, pl.ds(256 * i, 256), pl.ds(i * (rows - 2) * 128, 256)) for i in range(2)]
+    lanes = [pl.ds(0, 256), pl.ds(wide - 256, 256)]
+    own = (own0, own1)
+    ins = [[copies.start(o_in.at[there, lanes[s]], own[s].at[here, :]) for _, here, there in parts] for s in range(2)]
+    for s, (x, halo) in enumerate(((low, halo0), (high, halo1))):
+        ins[s].append(copies.start(x, halo))
+    out = []
+    for s, halo in enumerate((halo0, halo1)):
+        for c in ins[s]:
+            c.wait()
+        add_halo(tiles, wc, s, halo, own[s])
+        out += [copies.start(own[s].at[here, :], o_hbm.at[there, lanes[s]]) for _, here, there in parts]
+    for c in out:
+        c.wait()
+
+
+def corner_call(wc, low, high, out):
+    rows, wide = out.shape[0] // 128, out.shape[1]
+    vmem = pl.BlockSpec(memory_space=pltpu.VMEM)
+    return pl.pallas_call(
+        functools.partial(corner_kernel, wide // LANES, rows),
+        in_specs=[vmem] + [ANY] * 3,
+        out_specs=ANY,
         out_shape=jax.ShapeDtypeStruct(out.shape, F32),
+        scratch_shapes=[pltpu.VMEM(low.shape, F32)] * 4 + [pltpu.SemaphoreType.DMA((10,))],
         input_output_aliases={3: 0},
         compiler_params=params(),
-        cost_estimate=cost(count * height * 512 * 10, count * height * 512 * 12),
+        cost_estimate=cost(low.size * 20, low.size * 24),
     )(wc, low, high, out)
 
 
@@ -416,9 +502,15 @@
     up = lambda n: [(i, i + 1) for i in range(n - 1)]
     down = lambda n: [(i + 1, i) for i in range(n - 1)]
     wr, kr, wc = weights_call(rows, tiles, wind_direction, wind_speed, speed_table, diffusivity)
-    left, right = edge_call([cov], wr, kr, [(0, 0, rows, 0)], [(0, 0, 2, rows - 4)])
-    before = lax.ppermute(cov[-256:], "row", up(n_row))
-    after = lax.ppermute(cov[:256], "row", down(n_row))
+    sizes = chunks(rows - 4)
+    sizes[0] += 4
+    starts = [sum(sizes[:i]) for i in range(len(sizes))]
+    pieces = [(0, 128 * a, n, a) for a, n in zip(starts, sizes)]
+    left, right, first, final = edge_call(
+        [cov], wr, kr, pieces, [(0, 0, 2, rows - 4)], [[[i] for i in range(len(sizes))]], rims=True
+    )
+    before = lax.ppermute(final, "row", up(n_row))
+    after = lax.ppermute(first, "row", down(n_row))
     low = lax.ppermute(right, "col", up(n_col))
     high = lax.ppermute(left, "col", down(n_col))
     out, done = main_call(cov, wr, kr, wc)
@@ -428,13 +520,13 @@
         kr,
         [(0, 0, 2, 0), (1, 0, 4, 2), (1, 128 * (rows - 4), 4, 6), (2, 0, 2, 10)],
         [(0, 0, 0, 2), (6, 2, rows - 2, 2)],
+        [[[0, 1]], [[2, 3]]],
         [done],
     )
     low_c = lax.ppermute(right, "col", up(n_col))
     high_c = lax.ppermute(left, "col", down(n_col))
-    out = rim_call(cov, wr, kr, wc, before, after, out)
-    out = halo_call(out, wc, low, high, (128 * (rows - 4) // 2, 2), 256)
-    return halo_call(out, wc, low_c, high_c, (256, 2), 0, 128 * (rows - 2))
+    out = tail_call(cov, wr, kr, wc, before, after, low, high, out)
+    return corner_call(wc, low_c, high_c, out)
 
 
 def solution(mesh):

time: 168 us -> 149 us (0.89)
  Pallas kernels: 139 us -> 128 us
  local copies, waits for them, and re-layouts: 10.2 us -> 0.78 us
    pallas_call x5 -> x4, Pallas kernels: 62.4 us -> 55.5 us  [the longest x1 28.3 us: tail_call(): pl.pallas_call(functools.partial(tail_kernel, wide // LANES, rows), in_sp...]
    slice x1 -> x0, local copies, waits for them, and re-layouts: 4.76 us -> none  [local(): after = lax.ppermute(cov[:256], 'row', down(n_row))]
    unnamed x10 -> x2, local copies, waits for them, and re-layouts: 5.49 us -> 0.78 us
    pallas_call x1, Pallas kernels: 74.3 us -> 70.2 us  [main_call(): pl.pallas_call(functools.partial(main_kernel, wide // LANES), grid=(rows...]
  transfers between devices with their start and end apart: 6 -> 6, of which waited for: 0 -> 0; matrix products, arithmetic and copies ran while one was open for 3% -> 0% of each run, Pallas kernels for 68% -> 72%
where the time goes in v3:
time: 149 us; the launch traced here: 147 us
  Pallas kernels  128 us (86%)
  starting transfers between devices  18.3 us (12%)
    pallas_call x1, Pallas kernels, main_call(): pl.pallas_call(functools.partial(main_kernel, wide // LANES), grid=(rows...  70.2 us
    pallas_call x1, Pallas kernels, tail_call(): pl.pallas_call(functools.partial(tail_kernel, wide // LANES, rows), in_sp...  28.3 us
    pallas_call x2, Pallas kernels, edge_call(): pl.pallas_call(functools.partial(edge_kernel, pieces, runs, waits, len(so...  22.9 us
    ppermute x1, starting transfers between devices, local(): after = lax.ppermute(first, 'row', down(n_row))  5.33 us
    pallas_call x1, Pallas kernels, corner_call(): pl.pallas_call(functools.partial(corner_kernel, wide // LANES, rows), in_...  4.32 us
    ppermute x1, starting transfers between devices, local(): low_c = lax.ppermute(right, 'col', up(n_col))  3.69 us
    ppermute x1, starting transfers between devices, local(): low = lax.ppermute(right, 'col', up(n_col))  3.68 us
  transfers between devices with their start and end apart: 6, of which 0 were waited for; matrix products, arithmetic and copies ran while one was open for 0% of the time, Pallas kernels for 72%

profile of v3, /device:TPU:25, one launch (start us, length us, event | category | flops | bytes accessed | tf_op | source)
XLA Modules:
  0.0 146.9 jit_solution(5473903422887504616)
XLA Ops:
  0.0 2.1 %shard_map.55 = (f32[2,128,128]{2,1,0:T(8,128)}, f32[2,40,128]{2,1,0:T(8,128)}, f32[10,24,128]{2,1,0:T(8,128)}) custom-call(s32[2,16384]{1,0:T(2,128)} %wd.1, s32[2,16384]{1,0:T(2,128)} %ws.1, f32[2,8]{1,0:T(2,128)} %table.1, f32[128]{0:T(128)} %diff.1), custom_call_target="tpu_custom_call" | custom-call | flops 100000 | bytes 8388608 | tf_op jit(solution)/shard_map/pallas_call | solution.py:83
  2.1 15.4 %shard_map.56 = (f32[3584,256]{1,0:T(8,128)}, f32[3584,256]{1,0:T(8,128)}, f32[256,2048]{1,0:T(8,128)}, f32[256,2048]{1,0:T(8,128)}) custom-call(f32[2,128,128]{2,1,0:T(8,128)} %get-tuple-element.17.wr, f32[2,40,128]{2,1,0:T(8,128)} %get-tuple-element.18.kr, f32[4096,2048]{1,0:T(8,128)} %cov.1), custom_call_target="tpu_custom_call" | custom-call | flops 33030144 | bytes 14680064 | tf_op jit(solution)/shard_map/pallas_call | solution.py:231
  17.4 3.7 %collective-permute-start.4 = (f32[3584,256]{1,0:T(8,128)}, f32[3584,256]{1,0:T(8,128)}, u32[]{:S(2)}, u32[]{:S(2)}) collective-permute-start(f32[3584,256]{1,0:T(8,128)} %get-tuple-element.24), channel_id=1, source_target_pairs={{0,1},{1,2},{2,3},{3,4},{4,5},{5,6},{6,7},{8,9},{9,10},{10,11},{11... | collective-permute-start | bytes 11010056 | tf_op jit(solution)/shard_map/ppermute | solution.py:514
  21.1 2.4 %collective-permute-start.5 = (f32[3584,256]{1,0:T(8,128)}, f32[3584,256]{1,0:T(8,128)}, u32[]{:S(2)}, u32[]{:S(2)}) collective-permute-start(f32[3584,256]{1,0:T(8,128)} %get-tuple-element.25), channel_id=1, source_target_pairs={{1,0},{2,1},{3,2},{4,3},{5,4},{6,5},{7,6},{9,8},{10,9},{11,10},{12... | collective-permute-start | bytes 11010056 | tf_op jit(solution)/shard_map/ppermute | solution.py:515
  23.6 1.3 collective-permute-start
  24.9 5.3 %collective-permute-start.1 = (f32[256,2048]{1,0:T(8,128)}, f32[256,2048]{1,0:T(8,128)}, u32[]{:S(2)}, u32[]{:S(2)}) collective-permute-start(f32[256,2048]{1,0:T(8,128)} %get-tuple-element.20), channel_id=1, source_target_pairs={{8,0},{16,8},{24,16},{9,1},{17,9},{25,17},{10,2},{18,10},{26,18},{... | collective-permute-start | bytes 6291464 | tf_op jit(solution)/shard_map/ppermute | solution.py:513
  30.2 70.2 %shard_map.57 = (f32[4096,2048]{1,0:T(8,128)}, f32[8,128]{1,0:T(8,128)}) custom-call(f32[2,128,128]{2,1,0:T(8,128)} %get-tuple-element.17.wr, f32[2,40,128]{2,1,0:T(8,128)} %get-tuple-element.18.kr, f32[10,24,128]{2,1,0:T(8,128)} %get-tuple-element.16.wc, f32[4096,2048]{1,0:T(8,128)} %cov.1), custom_call_target="tpu_custom_call" | custom-call | flops 301989888 | bytes 67108864 | tf_op jit(solution)/shard_map/pallas_call | solution.py:353
  100.4 0.0 collective-permute-done.refs_0_.before
  100.4 0.0 collective-permute-done.1.refs_2_.after
  100.4 7.5 %shard_map.58 = (f32[512,256]{1,0:T(8,128)}, f32[512,256]{1,0:T(8,128)}) custom-call(f32[2,128,128]{2,1,0:T(8,128)} %get-tuple-element.17.wr, f32[2,40,128]{2,1,0:T(8,128)} %get-tuple-element.18.kr, f32[256,2048]{1,0:T(8,128)} %collective-permute-done.refs_0_.before, f32[4096,2048]{1,0:T(8,128)} %cov.1, f32[256,2048]{1,0:T(8,128)} %collective-permute-done.1.refs_2_.after, ...), custom_call_target="tpu_custom_call" | custom-call | flops 4718592 | bytes 2097152 | tf_op jit(solution)/shard_map/pallas_call | solution.py:231
  107.9 3.7 %collective-permute-start.2 = (f32[512,256]{1,0:T(8,128)}, f32[512,256]{1,0:T(8,128)S(1)}, u32[]{:S(2)}, u32[]{:S(2)}) collective-permute-start(f32[512,256]{1,0:T(8,128)} %get-tuple-element.22), channel_id=1, source_target_pairs={{0,1},{1,2},{2,3},{3,4},{4,5},{5,6},{6,7},{8,9},{9,10},{10,11},{11... | collective-permute-start | bytes 1572872 | tf_op jit(solution)/shard_map/ppermute | solution.py:526
  111.6 1.9 %collective-permute-start.3 = (f32[512,256]{1,0:T(8,128)}, f32[512,256]{1,0:T(8,128)}, u32[]{:S(2)}, u32[]{:S(2)}) collective-permute-start(f32[512,256]{1,0:T(8,128)} %get-tuple-element.23), channel_id=1, source_target_pairs={{1,0},{2,1},{3,2},{4,3},{5,4},{6,5},{7,6},{9,8},{10,9},{11,10},{12... | collective-permute-start | bytes 1572872 | tf_op jit(solution)/shard_map/ppermute | solution.py:527
  113.5 0.0 collective-permute-done.4.low
  113.5 0.0 collective-permute-done.5.high
  113.5 28.3 %shard_map.59.o_in = f32[4096,2048]{1,0:T(8,128)} custom-call(f32[2,128,128]{2,1,0:T(8,128)} %get-tuple-element.17.wr, f32[2,40,128]{2,1,0:T(8,128)} %get-tuple-element.18.kr, f32[10,24,128]{2,1,0:T(8,128)} %get-tuple-element.16.wc, f32[256,2048]{1,0:T(8,128)} %collective-permute-done.refs_0_.before, ...), custom_call_target="tpu_custom_call", output_to_operand_aliasing={{}: (8, {})} | custom-call | flops 67108864 | bytes 25165824 | tf_op jit(solution)/shard_map/pallas_call | solution.py:448
  141.8 0.0 collective-permute-done.2.low
  141.8 0.0 copy-start
  141.8 0.0 collective-permute-done.3.high
  141.8 0.8 copy-done
  142.6 4.3 %shard_map.60 = f32[4096,2048]{1,0:T(8,128)} custom-call(f32[10,24,128]{2,1,0:T(8,128)} %get-tuple-element.16.wc, f32[512,256]{1,0:T(8,128)} %copy-done, f32[512,256]{1,0:T(8,128)} %collective-permute-done.3.high, f32[4096,2048]{1,0:T(8,128)} %shard_map.59.o_in), custom_call_target="tpu_custom_call", output_to_operand_aliasing={{}: (3, {})} | custom-call | flops 2621440 | bytes 3145728 | tf_op jit(solution)/shard_map/pallas_call | solution.py:487
Async XLA Ops:
  17.4 96.1 %collective-permute-start.4 = (f32[3584,256]{1,0:T(8,128)}, f32[3584,256]{1,0:T(8,128)}, u32[]{:S(2)}, u32[]{:S(2)}) collective-permute-start(f32[3584,256]{1,0:T(8,128)} %get-tuple-element.24), channel_id=1, source_target_pairs={{0,1},{1,2},{2,3},{3,4},{4,5},{5,6},{6,7},{8,9},{9,10},{10,11},{11... | collective-permute-start | bytes 11010056 | tf_op jit(solution)/shard_map/ppermute | solution.py:514
  21.1 92.4 %collective-permute-start.5 = (f32[3584,256]{1,0:T(8,128)}, f32[3584,256]{1,0:T(8,128)}, u32[]{:S(2)}, u32[]{:S(2)}) collective-permute-start(f32[3584,256]{1,0:T(8,128)} %get-tuple-element.25), channel_id=1, source_target_pairs={{1,0},{2,1},{3,2},{4,3},{5,4},{6,5},{7,6},{9,8},{10,9},{11,10},{12... | collective-permute-start | bytes 11010056 | tf_op jit(solution)/shard_map/ppermute | solution.py:515
  23.6 76.8 %collective-permute-start = (f32[256,2048]{1,0:T(8,128)}, f32[256,2048]{1,0:T(8,128)}, u32[]{:S(2)}, u32[]{:S(2)}) collective-permute-start(f32[256,2048]{1,0:T(8,128)} %get-tuple-element.19), channel_id=1, source_target_pairs={{0,8},{8,16},{16,24},{1,9},{9,17},{17,25},{2,10},{10,18},{18,26},{... | collective-permute-start | bytes 6291464 | tf_op jit(solution)/shard_map/ppermute | solution.py:512
  24.9 75.5 %collective-permute-start.1 = (f32[256,2048]{1,0:T(8,128)}, f32[256,2048]{1,0:T(8,128)}, u32[]{:S(2)}, u32[]{:S(2)}) collective-permute-start(f32[256,2048]{1,0:T(8,128)} %get-tuple-element.20), channel_id=1, source_target_pairs={{8,0},{16,8},{24,16},{9,1},{17,9},{25,17},{10,2},{18,10},{26,18},{... | collective-permute-start | bytes 6291464 | tf_op jit(solution)/shard_map/ppermute | solution.py:513
  107.9 33.9 %collective-permute-start.2 = (f32[512,256]{1,0:T(8,128)}, f32[512,256]{1,0:T(8,128)S(1)}, u32[]{:S(2)}, u32[]{:S(2)}) collective-permute-start(f32[512,256]{1,0:T(8,128)} %get-tuple-element.22), channel_id=1, source_target_pairs={{0,1},{1,2},{2,3},{3,4},{4,5},{5,6},{6,7},{8,9},{9,10},{10,11},{11... | collective-permute-start | bytes 1572872 | tf_op jit(solution)/shard_map/ppermute | solution.py:526
  111.6 30.2 %collective-permute-start.3 = (f32[512,256]{1,0:T(8,128)}, f32[512,256]{1,0:T(8,128)}, u32[]{:S(2)}, u32[]{:S(2)}) collective-permute-start(f32[512,256]{1,0:T(8,128)} %get-tuple-element.23), channel_id=1, source_target_pairs={{1,0},{2,1},{3,2},{4,3},{5,4},{6,5},{7,6},{9,8},{10,9},{11,10},{12... | collective-permute-start | bytes 1572872 | tf_op jit(solution)/shard_map/ppermute | solution.py:527
  141.8 0.8 copy-start

commit v4 on v3

--- a/solution.py
+++ b/solution.py
@@ -11,7 +11,8 @@
 NLON = 128
 LANES = 128
 PAD = 8
-GROUPS = 2
+GROUPS = 16
+PART = 2
 F32 = jnp.float32
 ANY = pl.BlockSpec(memory_space=pl.ANY)
 
@@ -248,7 +249,7 @@
     return pltpu.roll(x, k, 1)
 
 
-def one_lat(tiles, slot, mode, index, f_ref, f_base, o_ref, o_base, next_weights, kr, wc, F, G, W):
+def one_lat(tiles, slot, mode, index, f_ref, f_base, o_ref, o_base, next_weights, kr, wc, F, G, W, H):
     Fs, F1, F2 = F[slot], F[(slot - 1) % 4], F[(slot - 2) % 4]
     G1, G2, G3 = G[(slot - 1) % 4], G[(slot - 2) % 4], G[(slot - 3) % 4]
     here, after = W[slot % 2], W[(slot + 1) % 2]
@@ -261,14 +262,11 @@
             for a in range(4):
                 after[a, pl.ds(r, 8), :] = jnp.broadcast_to(w[:, 32 * a + lane : 32 * a + lane + 1], (8, LANES))
 
-        def weights(sub):
+        def weights(sub, rs):
             k, whole = (jnp.broadcast_to(kr[a, pl.ds(index + 1 - sub, 1), :], (8, LANES)) for a in range(2))
             return [five(here[2 * sub, pl.ds(r, 8), :], here[2 * sub + 1, pl.ds(r, 8), :], k, whole) for r in rs]
 
-        w0 = weights(0) if mode >= 1 else None
-        w1 = weights(1) if mode >= 2 else None
-
-        def first(c):
+        def first(c, rs, w0):
             out = []
             for i, r in enumerate(rs):
                 x = f_ref[pl.ds(f_base + r, 8), c * LANES : (c + 1) * LANES]
@@ -286,8 +284,8 @@
                     out.append(g)
             return out
 
-        def second(c):
-            g = first(c)
+        def second(c, rs, w0, w1):
+            g = first(c, rs, w0)
             return [
                 w[0] * G2[c, pl.ds(PAD + r, 8), :]
                 + w[1] * G2[c, pl.ds(PAD - 1 + r, 8), :]
@@ -311,13 +309,21 @@
                 out.append(t)
             return out
 
+        for part in range(0, GROUPS, PART):
+            some = rs[part : part + PART]
+            w0 = weights(0, some) if mode >= 1 else None
+            w1 = weights(1, some) if mode >= 2 else None
+            for c in range(tiles):
+                if mode < 2:
+                    first(c, some, w0)
+                    continue
+                for i, x in enumerate(second(c, some, w0, w1)):
+                    H[c, 8 * (part + i) : 8 * (part + i) + 8, :] = x
         if mode < 2:
-            for c in range(tiles):
-                first(c)
             return
         h, u = {-2: None, -1: None}, {-2: None}
         for c in range(tiles + 2):
-            h[c] = second(c) if c < tiles else None
+            h[c] = [H[c, 8 * i : 8 * i + 8, :] for i in range(GROUPS)] if c < tiles else None
             u[c - 1] = across(0, c - 1, h[c - 1], h[c - 2], h[c])
             if c >= 2:
                 o = across(1, c - 2, u[c - 2], u[c - 3], u[c - 1])
@@ -330,14 +336,14 @@
 
 
 def main_kernel(tiles, wr, kr, wc, f_ref, o_ref, done, *ring):
-    F, G, W, turned = ring[:4], ring[4:8], ring[8:10], ring[10]
+    F, G, W, H, turned = ring[:4], ring[4:8], ring[8:10], ring[10], ring[11]
     t = pl.program_id(0)
     turned[...] = pltpu.roll(wr[(4 * t + 4) // 32], LANES - lax.rem(4 * t + 4, 32), 1)
 
     def four(modes):
         for q in range(4):
             next_weights = lambda r, q=q: (turned[pl.ds(r, 8), :], q)
-            one_lat(tiles, q, modes[q], 4 * t + q + 2, f_ref, 128 * q, o_ref, 128 * q, next_weights, kr, wc, F, G, W)
+            one_lat(tiles, q, modes[q], 4 * t + q + 2, f_ref, 128 * q, o_ref, 128 * q, next_weights, kr, wc, F, G, W, H)
 
     done[...] = jnp.zeros_like(done)
     pl.when(t == 0)(lambda: four((0, 0, 1, 1)))
@@ -345,7 +351,7 @@
 
 
 def rings(tiles):
-    return [pltpu.VMEM((tiles, 128 + 2 * PAD, LANES), F32)] * 8 + [pltpu.VMEM((4, 128, LANES), F32)] * 2
+    return [pltpu.VMEM((tiles, 128 + 2 * PAD, LANES), F32)] * 8 + [pltpu.VMEM((4, 128, LANES), F32)] * 2 + [pltpu.VMEM((tiles, 8 * GROUPS, LANES), F32)]
 
 
 def main_call(cov, wr, kr, wc):
@@ -380,19 +386,20 @@
     a = [weight(0, k, outer) for k in (0, 1, 2, way)]
     b = weight(0, way, edge)
     d = [weight(1, k, edge) for k in (0, 1, 2, way)]
-    e = weight(1, way, inner)
+    d = [d[0] * b, d[1] * roll(b, 1), d[2] * roll(b, LANES - 1), d[3]]
+    e = weight(1, way, inner) * b
 
     @pl.loop(0, halo.shape[0] // 128)
     def _(i):
         for j in range(16):
             at = pl.ds(pl.multiple_of(i * 128 + 8 * j, 8), 8)
             f1, f2 = halo[at, near : near + LANES], halo[at, far : far + LANES]
-            u1 = a[0] * f1 + a[1] * roll(f1, 1) + a[2] * roll(f1, LANES - 1) + a[3] * f2
-            u0 = b * f1
+            f_west, f_east = roll(f1, 1), roll(f1, LANES - 1)
+            u1 = a[0] * f1 + a[3] * f2 + a[1] * f_west + a[2] * f_east
             e_ref[at, at_edge : at_edge + LANES] = e_ref[at, at_edge : at_edge + LANES] + (
-                d[0] * u0 + d[1] * roll(u0, 1) + d[2] * roll(u0, LANES - 1) + d[3] * u1
+                d[0] * f1 + d[1] * f_west + d[2] * f_east + d[3] * u1
             )
-            e_ref[at, at_inner : at_inner + LANES] = e_ref[at, at_inner : at_inner + LANES] + e * u0
+            e_ref[at, at_inner : at_inner + LANES] = e_ref[at, at_inner : at_inner + LANES] + e * f1
 
 
 class Copies:
@@ -408,7 +415,7 @@
 
 def tail_kernel(tiles, rows, wr, kr, wc, before, after, low, high, cov, o_in, o_hbm, *scratch):
     halo, own, rim, side_halo, side_own = (scratch[2 * i : 2 * i + 2] for i in range(5))
-    F, G, W, sem = scratch[10:14], scratch[14:18], scratch[18:20], scratch[20]
+    F, G, W, H, sem = scratch[10:14], scratch[14:18], scratch[18:20], scratch[20], scratch[21]
     copies = Copies(sem)
     wide, size = tiles * LANES, (rows - 4) * 128
     inside = pl.ds(256, size)
@@ -431,7 +438,7 @@
         for q, (mode, (ref, base)) in enumerate(zip((0, 0, 1, 1, 2, 2), mine + theirs if i else theirs + mine)):
             at = index + q + 2
             next_weights = lambda r, at=at: (wr[at // 32, pl.ds(r, 8), :], at % 32)
-            one_lat(tiles, q % 4, mode, index + q, ref, base, rim[i], 128 * (q - 4), next_weights, kr, wc, F, G, W)
+            one_lat(tiles, q % 4, mode, index + q, ref, base, rim[i], 128 * (q - 4), next_weights, kr, wc, F, G, W, H)
         out.append(copies.start(rim[i], o_hbm.at[pl.ds(i * (rows - 2) * 128, 256), :]))
     for i in range(2):
         for c in ins[2 + i]:

time: 149 us -> 134 us (0.90)
  Pallas kernels: 128 us -> 104 us
  waiting for transfers between devices: 0.02 us -> 9.31 us
    pallas_call x1, Pallas kernels: 70.2 us -> 52.1 us  [main_call(): pl.pallas_call(functools.partial(main_kernel, wide // LANES), grid=(rows...]
    ppermute x1, waiting for transfers between devices: 0.01 us -> 9.29 us  [local(): high = lax.ppermute(left, 'col', down(n_col))]
    pallas_call x1, Pallas kernels: 28.3 us -> 22.5 us  [tail_call(): pl.pallas_call(functools.partial(tail_kernel, wide // LANES, rows), in_sp...]
  transfers between devices with their start and end apart: 6 -> 6, of which waited for: 0 -> 1; matrix products, arithmetic and copies ran while one was open for 0% -> 0% of each run, Pallas kernels for 72% -> 62%
where the time goes in v4:
time: 134 us; the launch traced here: 133 us
  Pallas kernels  104 us (78%)
  starting transfers between devices  18.6 us (14%)
  waiting for transfers between devices  9.31 us (7%)
    pallas_call x1, Pallas kernels, main_call(): pl.pallas_call(functools.partial(main_kernel, wide // LANES), grid=(rows...  52.1 us
    pallas_call x2, Pallas kernels, edge_call(): pl.pallas_call(functools.partial(edge_kernel, pieces, runs, waits, len(so...  22.9 us
    pallas_call x1, Pallas kernels, tail_call(): pl.pallas_call(functools.partial(tail_kernel, wide // LANES, rows), in_sp...  22.5 us
    ppermute x1, waiting for transfers between devices, local(): high = lax.ppermute(left, 'col', down(n_col))  9.29 us
    ppermute x1, starting transfers between devices, local(): after = lax.ppermute(first, 'row', down(n_row))  5.33 us
    pallas_call x1, Pallas kernels, corner_call(): pl.pallas_call(functools.partial(corner_kernel, wide // LANES, rows), in_...  4.4 us
    ppermute x1, starting transfers between devices, local(): low_c = lax.ppermute(right, 'col', up(n_col))  3.69 us
    ppermute x1, starting transfers between devices, local(): low = lax.ppermute(right, 'col', up(n_col))  3.68 us
  transfers between devices with their start and end apart: 6, of which 1 were waited for; matrix products, arithmetic and copies ran while one was open for 0% of the time, Pallas kernels for 62%

profile of v4, /device:TPU:25, one launch (start us, length us, event | category | flops | bytes accessed | tf_op | source)
XLA Modules:
  0.0 132.9 jit_solution(14388160763588104825)
XLA Ops:
  0.0 2.1 %shard_map.55 = (f32[2,128,128]{2,1,0:T(8,128)}, f32[2,40,128]{2,1,0:T(8,128)}, f32[10,24,128]{2,1,0:T(8,128)}) custom-call(s32[2,16384]{1,0:T(2,128)} %wd.1, s32[2,16384]{1,0:T(2,128)} %ws.1, f32[2,8]{1,0:T(2,128)} %table.1, f32[128]{0:T(128)} %diff.1), custom_call_target="tpu_custom_call" | custom-call | flops 100000 | bytes 8388608 | tf_op jit(solution)/shard_map/pallas_call | solution.py:84
  2.1 15.4 %shard_map.56 = (f32[3584,256]{1,0:T(8,128)}, f32[3584,256]{1,0:T(8,128)}, f32[256,2048]{1,0:T(8,128)}, f32[256,2048]{1,0:T(8,128)}) custom-call(f32[2,128,128]{2,1,0:T(8,128)} %get-tuple-element.17.wr, f32[2,40,128]{2,1,0:T(8,128)} %get-tuple-element.18.kr, f32[4096,2048]{1,0:T(8,128)} %cov.1), custom_call_target="tpu_custom_call" | custom-call | flops 33030144 | bytes 14680064 | tf_op jit(solution)/shard_map/pallas_call | solution.py:232
  17.4 3.7 %collective-permute-start.4 = (f32[3584,256]{1,0:T(8,128)}, f32[3584,256]{1,0:T(8,128)}, u32[]{:S(2)}, u32[]{:S(2)}) collective-permute-start(f32[3584,256]{1,0:T(8,128)} %get-tuple-element.24), channel_id=1, source_target_pairs={{0,1},{1,2},{2,3},{3,4},{4,5},{5,6},{6,7},{8,9},{9,10},{10,11},{11... | collective-permute-start | bytes 11010056 | tf_op jit(solution)/shard_map/ppermute | solution.py:521
  21.1 2.4 %collective-permute-start.5 = (f32[3584,256]{1,0:T(8,128)}, f32[3584,256]{1,0:T(8,128)}, u32[]{:S(2)}, u32[]{:S(2)}) collective-permute-start(f32[3584,256]{1,0:T(8,128)} %get-tuple-element.25), channel_id=1, source_target_pairs={{1,0},{2,1},{3,2},{4,3},{5,4},{6,5},{7,6},{9,8},{10,9},{11,10},{12... | collective-permute-start | bytes 11010056 | tf_op jit(solution)/shard_map/ppermute | solution.py:522
  23.6 1.3 collective-permute-start
  24.9 5.3 %collective-permute-start.1 = (f32[256,2048]{1,0:T(8,128)}, f32[256,2048]{1,0:T(8,128)}, u32[]{:S(2)}, u32[]{:S(2)}) collective-permute-start(f32[256,2048]{1,0:T(8,128)} %get-tuple-element.20), channel_id=1, source_target_pairs={{8,0},{16,8},{24,16},{9,1},{17,9},{25,17},{10,2},{18,10},{26,18},{... | collective-permute-start | bytes 6291464 | tf_op jit(solution)/shard_map/ppermute | solution.py:520
  30.2 52.1 %shard_map.57 = (f32[4096,2048]{1,0:T(8,128)}, f32[8,128]{1,0:T(8,128)}) custom-call(f32[2,128,128]{2,1,0:T(8,128)} %get-tuple-element.17.wr, f32[2,40,128]{2,1,0:T(8,128)} %get-tuple-element.18.kr, f32[10,24,128]{2,1,0:T(8,128)} %get-tuple-element.16.wc, f32[4096,2048]{1,0:T(8,128)} %cov.1), custom_call_target="tpu_custom_call" | custom-call | flops 301989888 | bytes 67108864 | tf_op jit(solution)/shard_map/pallas_call | solution.py:359
  82.3 0.0 collective-permute-done.refs_0_.before
  82.3 0.0 collective-permute-done.1.refs_2_.after
  82.3 7.5 %shard_map.58 = (f32[512,256]{1,0:T(8,128)}, f32[512,256]{1,0:T(8,128)}) custom-call(f32[2,128,128]{2,1,0:T(8,128)} %get-tuple-element.17.wr, f32[2,40,128]{2,1,0:T(8,128)} %get-tuple-element.18.kr, f32[256,2048]{1,0:T(8,128)} %collective-permute-done.refs_0_.before, f32[4096,2048]{1,0:T(8,128)} %cov.1, f32[256,2048]{1,0:T(8,128)} %collective-permute-done.1.refs_2_.after, ...), custom_call_target="tpu_custom_call" | custom-call | flops 4718592 | bytes 2097152 | tf_op jit(solution)/shard_map/pallas_call | solution.py:232
  89.9 3.7 %collective-permute-start.2 = (f32[512,256]{1,0:T(8,128)}, f32[512,256]{1,0:T(8,128)S(1)}, u32[]{:S(2)}, u32[]{:S(2)}) collective-permute-start(f32[512,256]{1,0:T(8,128)} %get-tuple-element.22), channel_id=1, source_target_pairs={{0,1},{1,2},{2,3},{3,4},{4,5},{5,6},{6,7},{8,9},{9,10},{10,11},{11... | collective-permute-start | bytes 1572872 | tf_op jit(solution)/shard_map/ppermute | solution.py:533
  93.6 2.1 %collective-permute-start.3 = (f32[512,256]{1,0:T(8,128)}, f32[512,256]{1,0:T(8,128)}, u32[]{:S(2)}, u32[]{:S(2)}) collective-permute-start(f32[512,256]{1,0:T(8,128)} %get-tuple-element.23), channel_id=1, source_target_pairs={{1,0},{2,1},{3,2},{4,3},{5,4},{6,5},{7,6},{9,8},{10,9},{11,10},{12... | collective-permute-start | bytes 1572872 | tf_op jit(solution)/shard_map/ppermute | solution.py:534
  95.7 0.0 collective-permute-done.4.low
  95.7 9.3 %collective-permute-done.5.high = f32[3584,256]{1,0:T(8,128)} collective-permute-done((f32[3584,256]{1,0:T(8,128)}, f32[3584,256]{1,0:T(8,128)}, u32[]{:S(2)}, u32[]{:S(2)}) %collective-permute-start.5) | collective-permute-done | bytes 3670048 | tf_op jit(solution)/shard_map/ppermute | solution.py:522
  105.0 22.5 %shard_map.59.o_in = f32[4096,2048]{1,0:T(8,128)} custom-call(f32[2,128,128]{2,1,0:T(8,128)} %get-tuple-element.17.wr, f32[2,40,128]{2,1,0:T(8,128)} %get-tuple-element.18.kr, f32[10,24,128]{2,1,0:T(8,128)} %get-tuple-element.16.wc, f32[256,2048]{1,0:T(8,128)} %collective-permute-done.refs_0_.before, ...), custom_call_target="tpu_custom_call", output_to_operand_aliasing={{}: (8, {})} | custom-call | flops 67108864 | bytes 25165824 | tf_op jit(solution)/shard_map/pallas_call | solution.py:455
  127.5 0.0 collective-permute-done.2.low
  127.5 0.0 copy-start
  127.5 0.0 collective-permute-done.3.high
  127.5 0.8 copy-done
  128.3 4.4 %shard_map.60 = f32[4096,2048]{1,0:T(8,128)} custom-call(f32[10,24,128]{2,1,0:T(8,128)} %get-tuple-element.16.wc, f32[512,256]{1,0:T(8,128)} %copy-done, f32[512,256]{1,0:T(8,128)} %collective-permute-done.3.high, f32[4096,2048]{1,0:T(8,128)} %shard_map.59.o_in), custom_call_target="tpu_custom_call", output_to_operand_aliasing={{}: (3, {})} | custom-call | flops 2621440 | bytes 3145728 | tf_op jit(solution)/shard_map/pallas_call | solution.py:494
Async XLA Ops:
  17.4 78.3 %collective-permute-start.4 = (f32[3584,256]{1,0:T(8,128)}, f32[3584,256]{1,0:T(8,128)}, u32[]{:S(2)}, u32[]{:S(2)}) collective-permute-start(f32[3584,256]{1,0:T(8,128)} %get-tuple-element.24), channel_id=1, source_target_pairs={{0,1},{1,2},{2,3},{3,4},{4,5},{5,6},{6,7},{8,9},{9,10},{10,11},{11... | collective-permute-start | bytes 11010056 | tf_op jit(solution)/shard_map/ppermute | solution.py:521
  21.1 83.9 %collective-permute-start.5 = (f32[3584,256]{1,0:T(8,128)}, f32[3584,256]{1,0:T(8,128)}, u32[]{:S(2)}, u32[]{:S(2)}) collective-permute-start(f32[3584,256]{1,0:T(8,128)} %get-tuple-element.25), channel_id=1, source_target_pairs={{1,0},{2,1},{3,2},{4,3},{5,4},{6,5},{7,6},{9,8},{10,9},{11,10},{12... | collective-permute-start | bytes 11010056 | tf_op jit(solution)/shard_map/ppermute | solution.py:522
  23.6 58.8 %collective-permute-start = (f32[256,2048]{1,0:T(8,128)}, f32[256,2048]{1,0:T(8,128)}, u32[]{:S(2)}, u32[]{:S(2)}) collective-permute-start(f32[256,2048]{1,0:T(8,128)} %get-tuple-element.19), channel_id=1, source_target_pairs={{0,8},{8,16},{16,24},{1,9},{9,17},{17,25},{2,10},{10,18},{18,26},{... | collective-permute-start | bytes 6291464 | tf_op jit(solution)/shard_map/ppermute | solution.py:519
  24.9 57.5 %collective-permute-start.1 = (f32[256,2048]{1,0:T(8,128)}, f32[256,2048]{1,0:T(8,128)}, u32[]{:S(2)}, u32[]{:S(2)}) collective-permute-start(f32[256,2048]{1,0:T(8,128)} %get-tuple-element.20), channel_id=1, source_target_pairs={{8,0},{16,8},{24,16},{9,1},{17,9},{25,17},{10,2},{18,10},{26,18},{... | collective-permute-start | bytes 6291464 | tf_op jit(solution)/shard_map/ppermute | solution.py:520
  89.9 37.6 %collective-permute-start.2 = (f32[512,256]{1,0:T(8,128)}, f32[512,256]{1,0:T(8,128)S(1)}, u32[]{:S(2)}, u32[]{:S(2)}) collective-permute-start(f32[512,256]{1,0:T(8,128)} %get-tuple-element.22), channel_id=1, source_target_pairs={{0,1},{1,2},{2,3},{3,4},{4,5},{5,6},{6,7},{8,9},{9,10},{10,11},{11... | collective-permute-start | bytes 1572872 | tf_op jit(solution)/shard_map/ppermute | solution.py:533
  93.6 34.0 %collective-permute-start.3 = (f32[512,256]{1,0:T(8,128)}, f32[512,256]{1,0:T(8,128)}, u32[]{:S(2)}, u32[]{:S(2)}) collective-permute-start(f32[512,256]{1,0:T(8,128)} %get-tuple-element.23), channel_id=1, source_target_pairs={{1,0},{2,1},{3,2},{4,3},{5,4},{6,5},{7,6},{9,8},{10,9},{11,10},{12... | collective-permute-start | bytes 1572872 | tf_op jit(solution)/shard_map/ppermute | solution.py:534
  127.5 0.8 copy-start
